TPU v7x, 128 devices: a whole 4x4x4 slice. The times are simulated.
128 devices in a mesh: dom: 128 (over y, z, x, core).
Axes of the slice: x: 4, y: 4, z: 4, core: 2. Of those that a mesh axis runs over, the one named last changes fastest.
Arguments:
- features: float32 [524288, 128], P('dom'), may hold values from -6 to 6
- owner: int32 [524288], P('dom'), may hold values from 0 to 127, as said below
- slot: int32 [524288], P('dom'), may hold values from 0 to 4095
- send_blocks: int32 [128, 128, 1], P('dom'), may hold values from 0 to 31
- tile_row: int32 [32768], P('dom'), may hold values from 0 to 31
- tile_col: int32 [32768], P('dom'), may hold values from 0 to 159
- tile_vals: int32 [32768, 128, 128], P('dom'), may hold values 0 or 1
- tile_count: int32 [128], P('dom'), may hold values from 64 to 256, as said below
- w_self1: bfloat16 [128, 256], replicated, may hold values from -0.5 to 0.5
- w_neigh1: bfloat16 [128, 256], replicated, may hold values from -4.21875 to 4.21875
- w_self2: bfloat16 [256, 256], replicated, may hold values from -0.375 to 0.375
- w_neigh2: bfloat16 [256, 256], replicated, may hold values from -3 to 3
Outputs:
- embed: bfloat16 [524288, 256], P('dom')
Inputs may be any that keep to these rules, and one draw needn't show every extreme that they name: Each partition's nodes in file order go exactly 4096 // 128 to every partition; the pairs (owner, slot) name every row of every partition once. `tile_count`: some partition uses all its tile slots.
All inputs are finite; a program needn't handle non-finite values. No bound on the sum of `tile_vals` on one device may be relied on, other than what follows from the above.
Results may differ from a plain program's by a relative error of at most 0.0043.
Values may be sent and summed in bfloat16 or wider, within the bound.
No kernel may reach another device: no remote copies, remote signals or barrier semaphores. Data moves between devices by JAX's collectives and lax.ppermute only.
A program may use at most 192 MiB of HBM per device.

v0:
```python
import jax
import jax.numpy as jnp
from jax import lax
from jax.sharding import PartitionSpec as P


def tile_sums(table, tile_vals_bf, tile_row, tile_col, valid, nblocks):
    chosen = table[tile_col]
    prod = jnp.einsum("tij,tjw->tiw", tile_vals_bf, chosen, preferred_element_type=jnp.float32)
    prod = prod * valid[:, None, None]
    return jnp.zeros((nblocks, table.shape[1], table.shape[2]), jnp.float32).at[tile_row].add(prod)


def local(
    features,
    owner,
    slot,
    send_blocks,
    tile_row,
    tile_col,
    tile_vals,
    tile_count,
    w_self1,
    w_neigh1,
    w_self2,
    w_neigh2,
):
    devices = lax.axis_size("dom")
    rows_local = features.shape[0]
    width_in = features.shape[1]
    blk = tile_vals.shape[1]
    nblocks = rows_local // blk
    width_hid = w_self1.shape[1]
    order = jnp.argsort(owner, stable=True)
    outgoing = features.astype(jnp.bfloat16)[order].reshape(
        devices, rows_local // devices, width_in
    )
    places = slot[order].reshape(devices, rows_local // devices)
    arrived, arrived_slots = (
        lax.all_to_all(outgoing, "dom", split_axis=0, concat_axis=0, tiled=True),
        lax.all_to_all(places, "dom", split_axis=0, concat_axis=0, tiled=True),
    )
    relaid = (
        jnp.zeros((rows_local, width_in), jnp.bfloat16)
        .at[arrived_slots.reshape(-1)]
        .set(arrived.reshape(rows_local, width_in))
    )
    valid = (jnp.arange(tile_vals.shape[0]) < tile_count[0]).astype(jnp.float32)
    tile_vals_bf = tile_vals.astype(jnp.bfloat16)
    row_sums = jnp.sum(tile_vals, axis=2).astype(jnp.float32) * valid[:, None]
    degree = jnp.zeros((nblocks, blk), jnp.float32).at[tile_row].add(row_sums)
    divisor = jnp.maximum(degree, 1.0)[:, :, None]
    picks = send_blocks[0]
    q_first = jnp.dot(relaid, w_neigh1, preferred_element_type=jnp.float32).astype(jnp.bfloat16)
    q_blocks = q_first.reshape(nblocks, blk, width_hid)
    incoming = lax.all_to_all(q_blocks[picks], "dom", split_axis=0, concat_axis=0, tiled=True)
    remote = incoming.reshape(-1, blk, width_hid)
    table = jnp.concatenate([q_blocks, remote], axis=0)
    agg_first = (
        tile_sums(table, tile_vals_bf, tile_row, tile_col, valid, nblocks) / divisor
    ).reshape(rows_local, width_hid)
    hidden = jax.nn.relu(
        jnp.dot(relaid, w_self1, preferred_element_type=jnp.float32) + agg_first
    ).astype(jnp.bfloat16)
    q_second = jnp.dot(hidden, w_neigh2, preferred_element_type=jnp.float32).astype(jnp.bfloat16)
    second_blocks = q_second.reshape(nblocks, blk, width_hid)
    incoming_second = lax.all_to_all(
        second_blocks[picks], "dom", split_axis=0, concat_axis=0, tiled=True
    )
    table_second = jnp.concatenate(
        [second_blocks, incoming_second.reshape(-1, blk, width_hid)], axis=0
    )
    agg_second = (
        tile_sums(table_second, tile_vals_bf, tile_row, tile_col, valid, nblocks) / divisor
    ).reshape(rows_local, width_hid)
    return (jnp.dot(hidden, w_self2, preferred_element_type=jnp.float32) + agg_second).astype(
        jnp.bfloat16
    )


def solution(mesh):
    placed = (
        P("dom", None),
        P("dom"),
        P("dom"),
        P("dom", None, None),
        P("dom"),
        P("dom"),
        P("dom", None, None),
        P("dom"),
        P(),
        P(),
        P(),
        P(),
    )
    return jax.shard_map(
        local, mesh=mesh, in_specs=placed, out_specs=P("dom", None), check_vma=False
    )
```

profile of v0, /device:TPU:1, one launch (start us, length us, event | category | flops | bytes accessed | tf_op | source)
XLA Modules:
  0.0 652.2 jit_solution(8133104319426316565)
XLA Ops:
  0.0 6.5 %sort.17 = (s32[4096]{0:T(1024)}, s32[4096]{0:T(1024)S(1)}) sort(s32[4096]{0:T(1024)} %param.13, s32[4096]{0:T(1024)S(1)} %iota.11), dimensions={0}, to_apply=%region_0.0 | sort | flops 49152 | bytes 65536 | tf_op jit(solution)/shard_map/jit(argsort)/sort | solution.py:34
  6.6 0.0 copy-start.5
  6.6 23.0 %gather_fusion = s32[4096]{0:T(1024)S(1)} fusion(s32[4096]{0:T(1024)S(1)} %copy-done.2, s32[4096]{0:T(1024)S(1)} %fusion.11), kind=kCustom, calls=%fused_computation | custom fusion | bytes 49152 | tf_op jit(solution)/shard_map/gather | solution.py:38
  29.6 0.0 copy-start.11
  29.6 0.0 copy-start.8
  29.6 0.7 all_to_all.15
  30.3 11.5 %all-to-all-start = ((s32[128,1,32]{2,1,0:T(1,128)}), s32[128,1,32]{2,1,0:T(1,128)S(1)}, u32[]{:S(2)}, u32[]{:S(2)}) async-start(s32[128,1,32]{2,1,0:T(1,128)} %bitcast), calls=%async_computation | async-start | bytes 131072 | tf_op jit(solution)/shard_map/all_to_all | solution.py:41
  41.8 0.0 copy-done.5
  41.8 0.1 convert_element_type.32
  42.0 15.0 %gather_fusion.1 = bf16[4096,128]{1,0:T(8,128)(2,1)} fusion(bf16[4096,128]{1,0:T(8,128)(2,1)S(1)} %convert_element_type.32, s32[4096]{0:T(1024)S(1)} %fusion.11), kind=kCustom, calls=%fused_computation.1 | custom fusion | bytes 2113536 | tf_op jit(solution)/shard_map/gather | solution.py:35
  57.0 0.0 all-to-all-done
  57.0 9.8 %all-to-all-start.1 = ((bf16[128,32,128]{2,1,0:T(8,128)(2,1)}), bf16[128,32,128]{2,1,0:T(8,128)(2,1)S(1)}, u32[]{:S(2)}, u32[]{:S(2)}) async-start(bf16[128,32,128]{2,1,0:T(8,128)(2,1)} %bitcast.2), calls=%async_computation.1 | async-start | bytes 2097152 | tf_op jit(solution)/shard_map/all_to_all | solution.py:40
  66.8 0.6 broadcast.112
  67.4 0.8 reduce.3
  68.3 0.1 reshape.110
  68.4 17.7 %all-to-all-done.1 = bf16[128,32,128]{2,1,0:T(8,128)(2,1)S(1)} async-done(((bf16[128,32,128]{2,1,0:T(8,128)(2,1)}), bf16[128,32,128]{2,1,0:T(8,128)(2,1)S(1)}, u32[]{:S(2)}, u32[]{:S(2)}) %all-to-all-start.1) | async-done | bytes 1048608 | tf_op jit(solution)/shard_map/all_to_all | solution.py:40
  86.1 11.1 %scatter_custom_fusion = bf16[4096,128]{1,0:T(8,128)(2,1)S(1)} fusion(s32[4096]{0:T(1024)S(1)} %bitcast.46, bf16[4096,128]{1,0:T(8,128)(2,1)S(1)} %bitcast.45, bf16[]{:T(256)} %constant.7.clone.1), kind=kCustom, calls=%fused_computation.25 | custom fusion | bytes 1048578 | tf_op jit(solution)/shard_map/scatter | solution.py:46
  97.2 0.0 copy-done.8
  97.3 0.7 convolution_convert_fusion
  97.9 6.6 %gather_fusion.2 = bf16[128,128,256]{2,1,0:T(8,128)(2,1)} fusion(bf16[32,128,256]{2,1,0:T(8,128)(2,1)S(1)} %bitcast.38, s32[1024]{0:T(1024)S(1)} %pad_clamp_fusion.1), kind=kCustom, calls=%fused_computation.2 | custom fusion | bytes 16777728 | tf_op jit(solution)/shard_map/gather | solution.py:56
  104.5 5.5 all-to-all-start.2
  110.7 0.0 copy-start.9
  110.7 0.0 copy-start.10
  110.7 8.2 %reduce_sum.9 = s32[256,128]{1,0:T(8,128)S(1)} reduce(s32[256,128,128]{2,1,0:T(8,128)} %param.18, s32[]{:T(128)} %constant.8.clone.1), dimensions={2}, to_apply=%region_3.4 | reduce | flops 4161536 | bytes 16908292 | tf_op jit(solution)/shard_map/reduce_sum | solution.py:50
  119.0 1.7 scatter_custom_fusion.2
  120.7 90.1 %all-to-all-done.2 = bf16[128,1,128,256]{3,2,1,0:T(8,128)(2,1)} async-done(((bf16[128,1,128,256]{3,2,1,0:T(8,128)(2,1)}), bf16[128,1,128,256]{3,2,1,0:T(8,128)(2,1)}, u32[]{:S(2)}, u32[]{:S(2)}) %all-to-all-start.2) | async-done | bytes 8388640 | tf_op jit(solution)/shard_map/all_to_all | solution.py:56
  210.8 8.7 %pad_maximum_fusion = bf16[160,128,256]{2,1,0:T(8,128)(2,1)} fusion(bf16[128,128,256]{2,1,0:T(8,128)(2,1)} %bitcast.9, bf16[32,128,256]{2,1,0:T(8,128)(2,1)S(1)} %bitcast.39), kind=kLoop, calls=%fused_computation.12 | loop fusion | flops 5242880 | bytes 20971520 | tf_op jit(solution)/shard_map/concatenate | solution.py:58
  219.5 13.7 %gather_fusion.3 = bf16[256,128,256]{2,1,0:T(8,128)(2,1)} fusion(bf16[160,128,256]{2,1,0:T(8,128)(2,1)} %pad_maximum_fusion, s32[1024]{0:T(1024)S(1)} %pad_clamp_fusion), kind=kCustom, calls=%fused_computation.3 | custom fusion | bytes 33555456 | tf_op jit(solution)/shard_map/gather | solution.py:8
  233.3 25.1 %multiply_bitcast_fusion.1 = f32[256,128,256]{1,2,0:T(8,128)} fusion(f32[256]{0:T(256)S(1)} %compare_convert_fusion, bf16[256,128,256]{2,1,0:T(8,128)(2,1)} %gather_fusion.3, s32[256,128,128]{2,1,0:T(8,128)} %param.18), kind=kOutput, calls=%fused_computation.11 | convolution fusion | flops 2160066560 | bytes 67109888 | tf_op jit(solution)/shard_map/tij,tjw->tiw/dot_general | solution.py:9
  258.4 33.4 %copy.22 = f32[256,128,256]{2,1,0:T(8,128)} copy(f32[256,128,256]{1,2,0:T(8,128)} %multiply_bitcast_fusion.1) | data formatting | bytes 67108864 | tf_op jit(solution)/shard_map/mul | solution.py:10
  291.8 2.5 broadcast.75.clone
  294.3 74.5 %scatter_fusion = f32[32,128,256]{2,1,0:T(8,128)} fusion(f32[32,128,256]{2,1,0:T(8,128)} %broadcast.75.clone, s32[256]{0:T(256)S(1)} %compare_select_fusion.3, f32[256,128,256]{2,1,0:T(8,128)} %copy.22), kind=kCustom, calls=%fused_computation.7 | custom fusion | flops 8388608 | bytes 100664320 | tf_op jit(solution)/shard_map/scatter-add | solution.py:11
  368.9 2.6 broadcast_divide_fusion.1
  371.5 0.7 fusion.1
  372.2 0.0 copy-start.3
  372.2 1.3 copy-done.3
  373.5 0.7 convolution_convert_fusion.1
  374.2 6.6 %gather_fusion.4 = bf16[128,128,256]{2,1,0:T(8,128)(2,1)} fusion(bf16[32,128,256]{2,1,0:T(8,128)(2,1)S(1)} %bitcast.36, s32[1024]{0:T(1024)S(1)} %pad_clamp_fusion.1), kind=kCustom, calls=%fused_computation.4 | custom fusion | bytes 16777728 | tf_op jit(solution)/shard_map/gather | solution.py:68
  380.8 110.8 %all_to_all.24 = bf16[128,1,128,256]{3,2,1,0:T(8,128)(2,1)S(1)} all-to-all(bf16[128,1,128,256]{3,2,1,0:T(8,128)(2,1)} %bitcast.41), channel_id=1, replica_groups=mesh['dom'=128] {'dom'}, dimensions={0} | all-to-all | bytes 16777216 | tf_op jit(solution)/shard_map/all_to_all | solution.py:67
  491.6 6.4 pad_maximum_fusion.1
  498.0 13.7 %gather_fusion.5 = bf16[256,128,256]{2,1,0:T(8,128)(2,1)} fusion(bf16[160,128,256]{2,1,0:T(8,128)(2,1)} %pad_maximum_fusion.1, s32[1024]{0:T(1024)S(1)} %pad_clamp_fusion), kind=kCustom, calls=%fused_computation.5 | custom fusion | bytes 33555456 | tf_op jit(solution)/shard_map/gather | solution.py:8
  511.7 25.1 %multiply_bitcast_fusion = f32[256,128,256]{1,2,0:T(8,128)} fusion(f32[256]{0:T(256)S(1)} %compare_convert_fusion, bf16[256,128,256]{2,1,0:T(8,128)(2,1)} %gather_fusion.5, s32[256,128,128]{2,1,0:T(8,128)} %param.18), kind=kOutput, calls=%fused_computation.10 | convolution fusion | flops 2160066560 | bytes 67109888 | tf_op jit(solution)/shard_map/tij,tjw->tiw/dot_general | solution.py:9
  536.8 33.4 %copy.25 = f32[256,128,256]{2,1,0:T(8,128)} copy(f32[256,128,256]{1,2,0:T(8,128)} %multiply_bitcast_fusion) | data formatting | bytes 67108864 | tf_op jit(solution)/shard_map/mul | solution.py:10
  570.2 2.5 broadcast.75
  572.8 74.5 %scatter_fusion.1 = f32[32,128,256]{2,1,0:T(8,128)} fusion(f32[32,128,256]{2,1,0:T(8,128)} %broadcast.75, s32[256]{0:T(256)S(1)} %compare_select_fusion.3, f32[256,128,256]{2,1,0:T(8,128)} %copy.25), kind=kCustom, calls=%fused_computation.9 | custom fusion | flops 8388608 | bytes 100664320 | tf_op jit(solution)/shard_map/scatter-add | solution.py:11
  647.3 2.7 broadcast_divide_fusion
  650.0 0.1 copy-done.4
  650.2 2.0 fusion.2
  (24 shorter events, 0.1 us)
Async XLA Ops:
  0.0 373.5 %copy-start = (bf16[256,256]{1,0:T(8,128)(2,1)S(1)}, bf16[256,256]{1,0:T(8,128)(2,1)}, u32[]{:S(2)}) copy-start(bf16[256,256]{1,0:T(8,128)(2,1)} %param.23) | copy-start | bytes 393220
  0.0 6.6 %copy-start.2 = (s32[4096]{0:T(1024)S(1)}, s32[4096]{0:T(1024)}, u32[]{:S(2)}) copy-start(s32[4096]{0:T(1024)} %param.14) | copy-start | bytes 49156
  6.6 35.3 %copy-start.5 = (f32[4096,128]{1,0:T(8,128)S(1)}, f32[4096,128]{1,0:T(8,128)}, u32[]{:S(2)}) copy-start(f32[4096,128]{1,0:T(8,128)} %param.12) | copy-start | bytes 6291460
  29.6 37.2 %copy-start.11 = (s32[1,128,1]{1,2,0:T(1,128)S(1)}, s32[1,128,1]{1,2,0:T(1,128)}, u32[]{:S(2)}) copy-start(s32[1,128,1]{1,2,0:T(1,128)} %param.15) | copy-start | bytes 1540
  29.6 67.6 %copy-start.8 = (bf16[128,256]{1,0:T(8,128)(2,1)S(1)}, bf16[128,256]{1,0:T(8,128)(2,1)}, u32[]{:S(2)}) copy-start(bf16[128,256]{1,0:T(8,128)(2,1)} %param.21) | copy-start | bytes 196612
  30.3 26.7 %all-to-all-start = ((s32[128,1,32]{2,1,0:T(1,128)}), s32[128,1,32]{2,1,0:T(1,128)S(1)}, u32[]{:S(2)}, u32[]{:S(2)}) async-start(s32[128,1,32]{2,1,0:T(1,128)} %bitcast), calls=%async_computation | async-start | bytes 131072 | tf_op jit(solution)/shard_map/all_to_all | solution.py:41
  57.0 29.1 %all-to-all-start.1 = ((bf16[128,32,128]{2,1,0:T(8,128)(2,1)}), bf16[128,32,128]{2,1,0:T(8,128)(2,1)S(1)}, u32[]{:S(2)}, u32[]{:S(2)}) async-start(bf16[128,32,128]{2,1,0:T(8,128)(2,1)} %bitcast.2), calls=%async_computation.1 | async-start | bytes 2097152 | tf_op jit(solution)/shard_map/all_to_all | solution.py:40
  104.5 106.3 %all-to-all-start.2 = ((bf16[128,1,128,256]{3,2,1,0:T(8,128)(2,1)}), bf16[128,1,128,256]{3,2,1,0:T(8,128)(2,1)}, u32[]{:S(2)}, u32[]{:S(2)}) async-start(bf16[128,1,128,256]{3,2,1,0:T(8,128)(2,1)} %bitcast.40), calls=%async_computation.2 | async-start | bytes 16777216 | tf_op jit(solution)/shard_map/all_to_all | solution.py:56
  110.7 8.3 %copy-start.9 = (s32[256]{0:T(256)S(1)}, s32[256]{0:T(256)}, u32[]{:S(2)}) copy-start(s32[256]{0:T(256)} %param.16) | copy-start | bytes 3076
  110.7 10.0 %copy-start.10 = (s32[256]{0:T(256)S(1)}, s32[256]{0:T(256)}, u32[]{:S(2)}) copy-start(s32[256]{0:T(256)} %param.17) | copy-start | bytes 3076
  368.9 2.6 copy-start.7
  372.2 1.3 copy-start.3
  572.8 79.4 %copy-start.1 = (bf16[256,256]{1,0:T(8,128)(2,1)S(1)}, bf16[256,256]{1,0:T(8,128)(2,1)}, u32[]{:S(2)}) copy-start(bf16[256,256]{1,0:T(8,128)(2,1)} %param.23) | copy-start | bytes 393220
  647.3 2.9 copy-start.4
  647.3 2.9 copy-start.6
where the time goes:
time: 654 us; the launch traced here: 652 us
  other arithmetic  187 us (29%)
  local copies, waits for them, and re-layouts  165 us (25%)
  blocking collectives  111 us (17%)
  waiting for transfers between devices  108 us (17%)
  matrix products  54.3 us (8%)
  starting transfers between devices  26.8 us (4%)
    scatter-add x2, other arithmetic, tile_sums(): jnp.zeros((nblocks, table.shape[1], table.shape[2]), jnp.float32)  149 us
    all_to_all x1, blocking collectives, local(): lax.all_to_all(second_blocks[picks], 'dom', split_axis=0, concat_axis=0,...  111 us
    all_to_all x1, waiting for transfers between devices, local(): lax.all_to_all(q_blocks[picks], 'dom', split_axis=0, concat_axis=0, tiled...  90.1 us
    mul x2, local copies, waits for them, and re-layouts, tile_sums(): prod = prod * valid[:, None, None]  66.9 us
    dot_general x2, matrix products, tile_sums(): jnp.einsum('tij,tjw->tiw', tile_vals_bf, chosen, preferred_element_type=j...  50.2 us
    gather x2, local copies, waits for them, and re-layouts, tile_sums(): chosen = table[tile_col]  27.5 us
    gather x1, local copies, waits for them, and re-layouts, local(): places = slot[order].reshape(devices, rows_local // devices)  23 us
    all_to_all x1, waiting for transfers between devices, local(): lax.all_to_all(outgoing, 'dom', split_axis=0, concat_axis=0, tiled=True)  17.7 us
  transfers between devices with their start and end apart: 3, of which 2 were waited for; matrix products, arithmetic and copies ran while one was open for 4% of the time, Pallas kernels for 0%

commit v1 on v0

v1 whole, which is shorter than its diff:
```python
import jax
import jax.numpy as jnp
from jax import lax
from jax.experimental import pallas as pl
from jax.experimental.pallas import tpu as pltpu
from jax.sharding import PartitionSpec as P

F = 128
H = 256
BLK = 128
ROWS = 4096
TILES = 256
NB = 32
ND = 128
PER = ROWS // ND
SEG = PER + 8
PAIRS = 176
GROUP = 8
UNROLL = 4
BF = jnp.bfloat16
F32 = jnp.float32
I32 = jnp.int32

SMEM = pl.BlockSpec(memory_space=pltpu.SMEM)
VMEM = pl.BlockSpec(memory_space=pltpu.VMEM)
ANY = pl.BlockSpec(memory_space=pl.ANY)


def params(mib):
    return pltpu.CompilerParams(vmem_limit_bytes=mib * 1024 * 1024)


def cost(flops, nbytes):
    return pl.CostEstimate(flops=flops, bytes_accessed=nbytes, transcendentals=0)


def mm(a, b):
    return jnp.dot(a, b, preferred_element_type=F32)


def mm_t(a, b):
    return lax.dot_general(a, b, (((1,), (1,)), ((), ())), preferred_element_type=F32)


def pack_kernel(owner, slot, feat, out, rows, pos_v, pos_s, sem):
    sub = lax.broadcasted_iota(I32, (BLK, BLK), 0)
    lane = lax.broadcasted_iota(I32, (BLK, BLK), 1)
    before = jnp.concatenate([(sub < lane).astype(BF), jnp.ones((BLK, BLK), BF)], axis=1)
    carry = jnp.zeros((BLK, BLK), F32)
    digits = jnp.zeros((BLK, BLK), F32)
    for c in range(ROWS // BLK):
        own = owner[c : c + 1, :]
        hit = own == sub
        hit_f = hit.astype(F32)
        counts = mm(hit_f.astype(BF), before)
        rank = jnp.sum(hit_f * (counts[:, :BLK] + carry), axis=0, keepdims=True)
        carry = carry + counts[:, BLK:]
        rank_i = rank.astype(I32)
        pos_v[c : c + 1, :] = own * SEG + rank_i
        places = slot[c : c + 1, :]
        high = (places >> 6).astype(F32)
        low = (places & 63).astype(F32)
        spread = jnp.concatenate([hit_f * high, hit_f * low], axis=1).astype(BF)
        ranks = jnp.concatenate([rank_i == sub, rank_i + PER == sub], axis=1).astype(F32).astype(BF)
        digits = digits + mm_t(spread, ranks)
    copy = pltpu.make_async_copy(pos_v, pos_s, sem)
    copy.start()
    rows.reshape(ND, SEG, F)[:, PER:, :] = jnp.broadcast_to(digits[:, None, :], (ND, SEG - PER, F))
    copy.wait()

    def move(i, _):
        c = i >> 3
        first = (i & 7) * 16
        for u in range(16):
            rows[pl.ds(pos_s[c, first + u], 1), :] = feat[pl.ds(i * 16 + u, 1), :]
        return 0

    lax.fori_loop(0, ROWS // 16, move, 0)
    out[...] = rows[...].reshape(ND, SEG, F).astype(BF)


def pack(features, owner, slot):
    return pl.pallas_call(
        pack_kernel,
        out_shape=jax.ShapeDtypeStruct((ND, SEG, F), BF),
        in_specs=[VMEM] * 3,
        out_specs=VMEM,
        scratch_shapes=[
            pltpu.VMEM((ND * SEG, F), F32),
            pltpu.VMEM((ROWS // BLK, BLK), I32),
            pltpu.SMEM((ROWS // BLK, BLK), I32),
            pltpu.SemaphoreType.DMA,
        ],
        compiler_params=params(24),
        name="pack",
    )(owner.reshape(ROWS // BLK, BLK), slot.reshape(ROWS // BLK, BLK), features)


def unpack_kernel(send_blocks, arrived, relaid, send, rows, placed, slot_v, slot_s, sem, sem_out):
    rows[...] = arrived[...].astype(F32).reshape(ND * SEG, F)
    digits = rows[pl.ds(PER, ND, stride=SEG), :]
    slot_v[...] = (digits * 64.0 + pltpu.roll(digits, F - PER, 1)).astype(I32)
    copy = pltpu.make_async_copy(slot_v, slot_s, sem)
    copy.start()
    copy.wait()

    def move(i, _):
        for u in range(PER):
            placed[pl.ds(slot_s[i, u], 1), :] = rows[pl.ds(i * SEG + u, 1), :]
        return 0

    lax.fori_loop(0, ND, move, 0)
    relaid[...] = placed[...].reshape(NB, BLK, F).astype(BF)

    def post(d, _):
        pltpu.make_async_copy(relaid.at[send_blocks[d]], send.at[d], sem_out).start()
        return 0

    lax.fori_loop(0, ND, post, 0)
    pltpu.make_async_copy(send, send, sem_out).wait()


def unpack(send_blocks, arrived):
    return pl.pallas_call(
        unpack_kernel,
        out_shape=(
            jax.ShapeDtypeStruct((NB, BLK, F), BF),
            jax.ShapeDtypeStruct((ND, BLK, F), BF),
        ),
        in_specs=[SMEM, VMEM],
        out_specs=(VMEM, ANY),
        scratch_shapes=[
            pltpu.VMEM((ND * SEG, F), F32),
            pltpu.VMEM((ROWS, F), F32),
            pltpu.VMEM((ND, F), I32),
            pltpu.SMEM((ND, F), I32),
            pltpu.SemaphoreType.DMA,
            pltpu.SemaphoreType.DMA,
        ],
        compiler_params=params(24),
        name="unpack",
    )(send_blocks, arrived)


def prepare_kernel(
    row_s, col_s, count_s, send_blocks, tile_vals, relaid,
    pairs, acc_out, inv_out, row_k, col_k, meta, dest, dest_at,
    tiles, acc, held, cursor, tile_k, sem,
):
    load = pltpu.make_async_copy(tile_vals, tiles.at[pl.ds(0, TILES)], sem)
    load.start()
    tiles[TILES] = jnp.zeros((BLK, BLK), I32)
    acc[...] = jnp.zeros_like(acc)

    def clear(i, _):
        cursor[i] = 0
        return 0

    lax.fori_loop(0, 2 * NB, clear, 0)

    def clear_pair(i, _):
        row_k[i] = 0
        for s in (0, 1):
            tile_k[2 * i + s] = TILES
            col_k[2 * i + s] = 0
        return 0

    lax.fori_loop(0, PAIRS, clear_pair, 0)
    used = count_s[0]

    def tally(t, _):
        g = row_s[t] + jnp.where(col_s[t] >= NB, NB, 0)
        cursor[g] = cursor[g] + 1
        return 0

    lax.fori_loop(0, used, tally, 0)

    def starts(g, at):
        n = cursor[g]
        cursor[g] = 2 * at
        return at + ((n + 1) >> 1)

    n_own = lax.fori_loop(0, NB, starts, 0)
    n_own = (n_own + GROUP - 1) // GROUP * GROUP
    n_all = lax.fori_loop(NB, 2 * NB, starts, n_own)
    n_all = (n_all + GROUP - 1) // GROUP * GROUP
    meta[0] = n_own
    meta[1] = n_all

    def place(t, _):
        row = row_s[t]
        col = col_s[t]
        far = col >= NB
        col = jnp.where(far, col - NB, col)
        g = row + jnp.where(far, NB, 0)
        at = cursor[g]
        cursor[g] = at + 1
        tile_k[at] = t
        col_k[at] = col
        row_k[at >> 1] = row
        return 0

    lax.fori_loop(0, used, place, 0)

    def zero_dest(i, _):
        cursor[i] = 0
        return 0

    lax.fori_loop(0, NB, zero_dest, 0)

    def tally_dest(d, _):
        b = send_blocks[d]
        cursor[b] = cursor[b] + 1
        return 0

    lax.fori_loop(0, ND, tally_dest, 0)

    def starts_dest(b, at):
        n = cursor[b]
        cursor[b] = at
        dest_at[b] = at
        return at + n

    dest_at[NB] = lax.fori_loop(0, NB, starts_dest, 0)

    def place_dest(d, _):
        b = send_blocks[d]
        at = cursor[b]
        cursor[b] = at + 1
        dest[at] = d
        return 0

    lax.fori_loop(0, ND, place_dest, 0)
    load.wait()
    ones = jnp.ones((2 * BLK, BLK), BF)

    def fetch(k):
        v = jnp.concatenate([tiles[tile_k[2 * k]], tiles[tile_k[2 * k + 1]]], axis=1)
        v = v.astype(F32).astype(BF)
        pairs[k] = v
        return v

    def own(i, _):
        for u in range(UNROLL):
            k = i * UNROLL + u
            v = fetch(k)
            x = jnp.concatenate([relaid[col_k[2 * k]], relaid[col_k[2 * k + 1]]], axis=0)
            got = mm(v, jnp.concatenate([x, ones], axis=1))
            acc[row_k[k]] += got
        return 0

    lax.fori_loop(0, n_own // UNROLL, own, 0)

    def far(i, _):
        for u in range(UNROLL):
            k = i * UNROLL + u
            r = row_k[k]
            acc[r, :, BLK:] += mm(fetch(k), ones)
        return 0

    lax.fori_loop(n_own // UNROLL, n_all // UNROLL, far, 0)
    acc_out[...] = acc[:, :, :BLK]
    inv_out[...] = 1.0 / jnp.maximum(acc[:, :, BLK:], 1.0)


def prepare(tile_row, tile_col, tile_count, send_blocks, tile_vals, relaid):
    ints = lambda n: jax.ShapeDtypeStruct((n,), I32)
    return pl.pallas_call(
        prepare_kernel,
        out_shape=(
            jax.ShapeDtypeStruct((PAIRS, BLK, 2 * BLK), BF),
            jax.ShapeDtypeStruct((NB, BLK, F), F32),
            jax.ShapeDtypeStruct((NB, BLK, BLK), F32),
            ints(PAIRS),
            ints(2 * PAIRS),
            ints(8),
            ints(ND),
            ints(NB + 8),
        ),
        in_specs=[SMEM, SMEM, SMEM, SMEM, ANY, VMEM],
        out_specs=(VMEM, VMEM, VMEM, SMEM, SMEM, SMEM, SMEM, SMEM),
        scratch_shapes=[
            pltpu.VMEM((TILES + 1, BLK, BLK), I32),
            pltpu.VMEM((NB, BLK, 2 * BLK), F32),
            pltpu.VMEM((8, BLK), F32),
            pltpu.SMEM((2 * NB,), I32),
            pltpu.SMEM((2 * PAIRS,), I32),
            pltpu.SemaphoreType.DMA,
        ],
        compiler_params=params(48),
        cost_estimate=cost(2 * 10**9, 32 * 2**20),
        name="prepare",
    )(tile_row, tile_col, tile_count, send_blocks, tile_vals, relaid)


def add_pairs(first, last, start, held, sems, table, acc, row_k, col_k):
    def group(c, _):
        pltpu.make_async_copy(held.at[pl.ds(0, GROUP)], held.at[pl.ds(0, GROUP)], sems.at[c]).wait()
        for u0 in range(0, GROUP, UNROLL):
            for u in range(u0, u0 + UNROLL):
                k = first + c * GROUP + u
                x = jnp.concatenate([table[col_k[2 * k]], table[col_k[2 * k + 1]]], axis=0)
                got = mm(held[c * GROUP + u], x)
                acc[row_k[k]] += got
        return 0

    lax.fori_loop(0, (last - first) // GROUP, group, 0)


def load_pairs(first, last, pairs, held, sems):
    def group(c, _):
        pltpu.make_async_copy(
            pairs.at[pl.ds(first + c * GROUP, GROUP)], held.at[pl.ds(c * GROUP, GROUP)], sems.at[c]
        ).start()
        return 0

    lax.fori_loop(0, (last - first) // GROUP, group, 0)


def first_kernel(
    row_k, col_k, meta, dest, dest_at, pairs, remote, relaid, acc_in, inv, w_self, w_neigh, w_next,
    hidden, q_out, send,
    held, acc, sems, sem_out,
):
    n_own = meta[0]
    n_all = meta[1]
    load_pairs(n_own, n_all, pairs, held, sems)
    acc[...] = acc_in[...]
    add_pairs(n_own, n_all, 0, held, sems, remote, acc, row_k, col_k)
    weights = jnp.concatenate([w_self[...], w_neigh[...], w_neigh[...]], axis=0)

    def finish(i, _):
        b = pl.ds(2 * i, 2)
        mean = (acc[b] * inv[b]).reshape(2 * BLK, F)
        high = mean.astype(BF)
        low = (mean - high.astype(F32)).astype(BF)
        x = jnp.concatenate([relaid[b].reshape(2 * BLK, F), high, low], axis=1)
        h = jnp.maximum(mm(x, weights), 0.0).astype(BF)
        hidden[b] = h.reshape(2, BLK, H)
        q_out[b] = mm(h, w_next[...]).astype(BF).reshape(2, BLK, H)

        def post(j, _):
            d = dest[j]
            blk = 2 * i + jnp.where(j >= dest_at[2 * i + 1], 1, 0)
            pltpu.make_async_copy(q_out.at[blk], send.at[d], sem_out).start()
            return 0

        lax.fori_loop(dest_at[2 * i], dest_at[2 * i + 2], post, 0)
        return 0

    lax.fori_loop(0, NB // 2, finish, 0)
    pltpu.make_async_copy(send, send, sem_out).wait()


def first(lists, pairs, remote, relaid, acc, inv, w_self, w_neigh, w_next):
    row_k, col_k, meta, dest, dest_at = lists
    return pl.pallas_call(
        first_kernel,
        out_shape=(
            jax.ShapeDtypeStruct((NB, BLK, H), BF),
            jax.ShapeDtypeStruct((NB, BLK, H), BF),
            jax.ShapeDtypeStruct((ND, BLK, H), BF),
        ),
        in_specs=[SMEM] * 5 + [ANY] + [VMEM] * 7,
        out_specs=(VMEM, VMEM, ANY),
        scratch_shapes=[
            pltpu.VMEM((PAIRS, BLK, 2 * BLK), BF),
            pltpu.VMEM((NB, BLK, F), F32),
            pltpu.SemaphoreType.DMA((PAIRS // GROUP,)),
            pltpu.SemaphoreType.DMA,
        ],
        compiler_params=params(48),
        name="first_layer",
    )(row_k, col_k, meta, dest, dest_at, pairs, remote, relaid, acc, inv, w_self, w_neigh, w_next)


def own_kernel(row_k, col_k, meta, pairs, q, hidden, inv, w_self, base, held, acc, sems):
    n_own = meta[0]
    load_pairs(0, n_own, pairs, held, sems)
    acc[...] = jnp.zeros_like(acc)
    add_pairs(0, n_own, 0, held, sems, q, acc, row_k, col_k)

    def finish(b, _):
        scale = inv[b]
        base[b] = mm(hidden[b], w_self[...]) + acc[b] * jnp.concatenate([scale, scale], axis=1)
        return 0

    lax.fori_loop(0, NB, finish, 0)


def own_part(lists, pairs, q, hidden, inv, w_self):
    row_k, col_k, meta, _, _ = lists
    return pl.pallas_call(
        own_kernel,
        out_shape=jax.ShapeDtypeStruct((NB, BLK, H), F32),
        in_specs=[SMEM] * 3 + [ANY] + [VMEM] * 4,
        out_specs=VMEM,
        scratch_shapes=[
            pltpu.VMEM((PAIRS, BLK, 2 * BLK), BF),
            pltpu.VMEM((NB, BLK, H), F32),
            pltpu.SemaphoreType.DMA((PAIRS // GROUP,)),
        ],
        compiler_params=params(48),
        cost_estimate=cost(2 * 10**9, 32 * 2**20),
        name="own_part",
    )(row_k, col_k, meta, pairs, q, hidden, inv, w_self)


def second_kernel(row_k, col_k, meta, pairs, remote, base, inv, out, held, acc, sems):
    n_own = meta[0]
    n_all = meta[1]
    load_pairs(n_own, n_all, pairs, held, sems)
    acc[...] = jnp.zeros_like(acc)
    add_pairs(n_own, n_all, 0, held, sems, remote, acc, row_k, col_k)

    def finish(b, _):
        scale = inv[b]
        out[b] = (base[b] + acc[b] * jnp.concatenate([scale, scale], axis=1)).astype(BF)
        return 0

    lax.fori_loop(0, NB, finish, 0)


def second(lists, pairs, remote, base, inv):
    row_k, col_k, meta, _, _ = lists
    return pl.pallas_call(
        second_kernel,
        out_shape=jax.ShapeDtypeStruct((NB, BLK, H), BF),
        in_specs=[SMEM] * 3 + [ANY] + [VMEM] * 3,
        out_specs=VMEM,
        scratch_shapes=[
            pltpu.VMEM((PAIRS, BLK, 2 * BLK), BF),
            pltpu.VMEM((NB, BLK, H), F32),
            pltpu.SemaphoreType.DMA((PAIRS // GROUP,)),
        ],
        compiler_params=params(48),
        name="second_layer",
    )(row_k, col_k, meta, pairs, remote, base, inv)


def exchange(x):
    return lax.all_to_all(x, "dom", split_axis=0, concat_axis=0, tiled=True)


def local(
    features, owner, slot, send_blocks, tile_row, tile_col, tile_vals, tile_count,
    w_self1, w_neigh1, w_self2, w_neigh2,
):
    picks = send_blocks.reshape(ND)
    arrived = exchange(pack(features, owner, slot))
    relaid, send = unpack(picks, arrived)
    remote = exchange(send)
    pairs, acc, inv, *lists = prepare(tile_row, tile_col, tile_count, picks, tile_vals, relaid)
    hidden, q, send = first(lists, pairs, remote, relaid, acc, inv, w_self1, w_neigh1, w_neigh2)
    remote = exchange(send)
    base = own_part(lists, pairs, q, hidden, inv, w_self2)
    return second(lists, pairs, remote, base, inv).reshape(ROWS, H)


def solution(mesh):
    rows, flat = P("dom", None), P("dom")
    cube = P("dom", None, None)
    placed = (rows, flat, flat, cube, flat, flat, cube, flat, P(), P(), P(), P())
    return jax.shard_map(local, mesh=mesh, in_specs=placed, out_specs=rows, check_vma=False)
```

time: 654 us -> 263 us (0.40)
  the two profiles are of different devices: /device:TPU:1 before, /device:TPU:19 now
where the time goes in v1:
time: 263 us; the launch traced here: 262 us
  waiting for transfers between devices  110 us (42%)
  Pallas kernels  91.4 us (35%)
  blocking collectives  29.2 us (11%)
  starting transfers between devices  17.6 us (7%)
  local copies, waits for them, and re-layouts  13.6 us (5%)
    all_to_all x2, waiting for transfers between devices, exchange(): return lax.all_to_all(x, 'dom', split_axis=0, concat_axis=0, tiled=True)  110 us
    all_to_all x1, blocking collectives, exchange(): return lax.all_to_all(x, 'dom', split_axis=0, concat_axis=0, tiled=True)  29.2 us
    pallas_call x1, Pallas kernels, prepare(): pl.pallas_call(prepare_kernel, out_shape=(jax.ShapeDtypeStruct((PAIRS, BL...  25.3 us
    all_to_all x2, starting transfers between devices, exchange(): return lax.all_to_all(x, 'dom', split_axis=0, concat_axis=0, tiled=True)  17.6 us
    pallas_call x1, Pallas kernels, first(): pl.pallas_call(first_kernel, out_shape=(jax.ShapeDtypeStruct((NB, BLK, H)...  16.6 us
    unnamed x36, local copies, waits for them, and re-layouts  13.6 us
    pallas_call x1, Pallas kernels, unpack(): pl.pallas_call(unpack_kernel, out_shape=(jax.ShapeDtypeStruct((NB, BLK, F...  12.8 us
    pallas_call x1, Pallas kernels, own_part(): pl.pallas_call(own_kernel, out_shape=jax.ShapeDtypeStruct((NB, BLK, H), F...  12.6 us
  transfers between devices with their start and end apart: 2, of which 2 were waited for; matrix products, arithmetic and copies ran while one was open for 0% of the time, Pallas kernels for 14%

profile of v1, /device:TPU:19, one launch (start us, length us, event | category | flops | bytes accessed | tf_op | source)
XLA Modules:
  0.0 262.3 jit_solution(12072681824125560655)
XLA Ops:
  0.0 0.0 copy-start.8
  0.0 1.6 copy-done.8
  1.6 0.0 copy-start.13
  1.6 0.7 copy-done.13
  2.3 0.0 copy-start.14
  2.3 0.7 copy-done.14
  3.0 12.4 %pack.1 = bf16[128,40,128]{2,1,0:T(8,128)(2,1)S(1)} custom-call(s32[32,128]{1,0:T(8,128)S(1)} %bitcast.4, s32[32,128]{1,0:T(8,128)S(1)} %bitcast.5, f32[4096,128]{1,0:T(8,128)S(1)} %copy-done.8), custom_call_target="tpu_custom_call" | custom-call | tf_op jit(solution)/shard_map/pack/pallas_call | solution.py:83
  15.5 0.0 copy-start.15
  15.5 29.2 %all_to_all.15.arrived = bf16[128,40,128]{2,1,0:T(8,128)(2,1)S(1)} all-to-all(bf16[128,40,128]{2,1,0:T(8,128)(2,1)S(1)} %pack.1), channel_id=1, replica_groups=mesh['dom'=128] {'dom'}, dimensions={0} | all-to-all | bytes 2621440 | tf_op jit(solution)/shard_map/all_to_all | solution.py:442
  44.7 0.0 copy-done.15
  44.7 12.8 %unpack.1 = (bf16[32,128,128]{2,1,0:T(8,128)(2,1)S(1)}, bf16[128,128,128]{2,1,0:T(8,128)(2,1)S(1)}) custom-call(s32[128]{0:T(128)S(1)} %bitcast.6, bf16[128,40,128]{2,1,0:T(8,128)(2,1)S(1)} %all_to_all.15.arrived), custom_call_target="tpu_custom_call" | custom-call | tf_op jit(solution)/shard_map/unpack/pallas_call | solution.py:124
  57.6 0.0 copy-start.2
  57.6 1.9 copy-done.2
  59.5 0.0 copy-start.16
  59.5 0.0 copy-start.17
  59.5 9.0 %all-to-all-start.1 = ((bf16[128,128,128]{2,1,0:T(8,128)(2,1)}), bf16[128,128,128]{2,1,0:T(8,128)(2,1)}, u32[]{:S(2)}, u32[]{:S(2)}) async-start(bf16[128,128,128]{2,1,0:T(8,128)(2,1)} %copy-done.2), calls=%async_computation.1 | async-start | bytes 8388608 | tf_op jit(solution)/shard_map/all_to_all | solution.py:442
  69.2 0.0 copy-done.16
  69.2 0.0 copy-done.17
  69.2 0.0 copy-start.9
  69.3 0.0 copy-start.11
  69.3 0.0 copy-start.12
  69.3 25.3 %prepare.1 = (bf16[176,128,256]{2,1,0:T(8,128)(2,1)}, f32[32,128,128]{2,1,0:T(8,128)S(1)}, f32[32,128,128]{2,1,0:T(8,128)S(1)}, s32[176]{0:T(256)S(1)}, s32[352]...) custom-call(s32[256]{0:T(256)S(1)} %copy-done.16, s32[256]{0:T(256)S(1)} %copy-done.17, ...), custom_call_target="tpu_custom_call" | custom-call | flops 2000000000 | bytes 33554432 | tf_op jit(solution)/shard_map/prepare/pallas_call | solution.py:268
  94.6 0.0 copy-start
  94.6 1.3 copy-done
  95.9 0.0 copy-start.3
  95.9 1.3 copy-done.3
  97.3 20.7 %all-to-all-done.1.remote = bf16[128,128,128]{2,1,0:T(8,128)(2,1)} async-done(((bf16[128,128,128]{2,1,0:T(8,128)(2,1)}), bf16[128,128,128]{2,1,0:T(8,128)(2,1)}, u32[]{:S(2)}, u32[]{:S(2)}) %all-to-all-start.1) | async-done | bytes 4194336 | tf_op jit(solution)/shard_map/all_to_all | solution.py:442
  118.0 0.0 copy-done.9
  118.0 0.0 copy-done.11
  118.0 0.0 copy-done.12
  118.0 16.6 %first_layer.1 = (bf16[32,128,256]{2,1,0:T(8,128)(2,1)S(1)}, bf16[32,128,256]{2,1,0:T(8,128)(2,1)S(1)}, bf16[128,128,256]{2,1,0:T(8,128)(2,1)}) custom-call(s32[176]{0:T(256)S(1)} %get-tuple-element.19.row_k, s32[352]{0:T(512)S(1)} %get-tuple-element.20.col_k, s32[8]{0:T(128)S(1)} %get-tuple-element.21.meta, s32[128]{0:T(128)S(1)} %get-tuple-element.23.dest, ...), custom_call_target="tpu_custom_call" | custom-call | tf_op jit(solution)/shard_map/first_layer/pallas_call | solution.py:357
  134.6 0.0 copy-start.4
  134.6 1.4 copy-done.4
  136.0 0.0 copy-start.6
  136.0 1.3 copy-done.6
  137.3 0.0 copy-start.10
  137.3 8.6 %all-to-all-start.2 = ((bf16[128,128,256]{2,1,0:T(8,128)(2,1)}), bf16[128,128,256]{2,1,0:T(8,128)(2,1)}, u32[]{:S(2)}, u32[]{:S(2)}) async-start(bf16[128,128,256]{2,1,0:T(8,128)(2,1)} %get-tuple-element.28), calls=%async_computation.2 | async-start | bytes 16777216 | tf_op jit(solution)/shard_map/all_to_all | solution.py:442
  146.0 0.0 copy-done.10
  146.0 0.0 copy-start.5
  146.0 1.6 copy-done.5
  147.6 0.0 copy-start.7
  147.6 1.6 copy-done.7
  149.2 0.0 copy-start.1
  149.2 12.6 %own_part.1.base = f32[32,128,256]{2,1,0:T(8,128)} custom-call(s32[176]{0:T(256)S(1)} %get-tuple-element.19.row_k, s32[352]{0:T(512)S(1)} %get-tuple-element.20.col_k, s32[8]{0:T(128)S(1)} %get-tuple-element.21.meta, bf16[176,128,256]{2,1,0:T(8,128)(2,1)} %get-tuple-element.22.pairs, bf16[32,128,256]{2,1,0:T(8,128)(2,1)S(1)} %copy-done.7, ...), custom_call_target="tpu_custom_call" | custom-call | flops 2000000000 | bytes 33554432 | tf_op jit(solution)/shard_map/own_part/pallas_call | solution.py:393
  161.8 89.0 %all-to-all-done.2.remote = bf16[128,128,256]{2,1,0:T(8,128)(2,1)} async-done(((bf16[128,128,256]{2,1,0:T(8,128)(2,1)}), bf16[128,128,256]{2,1,0:T(8,128)(2,1)}, u32[]{:S(2)}, u32[]{:S(2)}) %all-to-all-start.2) | async-done | bytes 8388640 | tf_op jit(solution)/shard_map/all_to_all | solution.py:442
  250.8 0.0 copy-done.1
  250.8 11.6 %second_layer.1 = bf16[32,128,256]{2,1,0:T(8,128)(2,1)} custom-call(s32[176]{0:T(256)S(1)} %get-tuple-element.19.row_k, s32[352]{0:T(512)S(1)} %get-tuple-element.20.col_k, s32[8]{0:T(128)S(1)} %get-tuple-element.21.meta, bf16[176,128,256]{2,1,0:T(8,128)(2,1)} %get-tuple-element.22.pairs, bf16[128,128,256]{2,1,0:T(8,128)(2,1)} %all-to-all-done.2.remote, ...), custom_call_target="tpu_custom_call" | custom-call | tf_op jit(solution)/shard_map/second_layer/pallas_call | solution.py:426
Async XLA Ops:
  0.0 1.6 copy-start.8
  1.6 0.7 copy-start.13
  2.3 0.7 copy-start.14
  15.5 29.3 %copy-start.15 = (s32[1,128,1]{1,2,0:T(1,128)S(1)}, s32[1,128,1]{1,2,0:T(1,128)}, u32[]{:S(2)}) copy-start(s32[1,128,1]{1,2,0:T(1,128)} %param.15) | copy-start | bytes 1540
  57.6 1.9 copy-start.2
  59.5 9.7 %copy-start.16 = (s32[256]{0:T(256)S(1)}, s32[256]{0:T(256)}, u32[]{:S(2)}) copy-start(s32[256]{0:T(256)} %row_s.1) | copy-start | bytes 3076
  59.5 9.7 %copy-start.17 = (s32[256]{0:T(256)S(1)}, s32[256]{0:T(256)}, u32[]{:S(2)}) copy-start(s32[256]{0:T(256)} %col_s.1) | copy-start | bytes 3076
  59.5 58.4 %all-to-all-start.1 = ((bf16[128,128,128]{2,1,0:T(8,128)(2,1)}), bf16[128,128,128]{2,1,0:T(8,128)(2,1)}, u32[]{:S(2)}, u32[]{:S(2)}) async-start(bf16[128,128,128]{2,1,0:T(8,128)(2,1)} %copy-done.2), calls=%async_computation.1 | async-start | bytes 8388608 | tf_op jit(solution)/shard_map/all_to_all | solution.py:442
  69.2 48.7 %copy-start.9 = (bf16[256,256]{1,0:T(8,128)(2,1)S(1)}, bf16[256,256]{1,0:T(8,128)(2,1)}, u32[]{:S(2)}) copy-start(bf16[256,256]{1,0:T(8,128)(2,1)} %w_next.1) | copy-start | bytes 393220
  69.3 48.7 %copy-start.11 = (bf16[128,256]{1,0:T(8,128)(2,1)S(1)}, bf16[128,256]{1,0:T(8,128)(2,1)}, u32[]{:S(2)}) copy-start(bf16[128,256]{1,0:T(8,128)(2,1)} %w_self.2) | copy-start | bytes 196612
  69.3 48.7 %copy-start.12 = (bf16[128,256]{1,0:T(8,128)(2,1)S(1)}, bf16[128,256]{1,0:T(8,128)(2,1)}, u32[]{:S(2)}) copy-start(bf16[128,256]{1,0:T(8,128)(2,1)} %w_neigh.1) | copy-start | bytes 196612
  94.6 1.3 copy-start
  95.9 1.3 copy-start.3
  134.6 1.4 copy-start.4
  136.0 1.3 copy-start.6
  137.3 8.6 %copy-start.10 = (bf16[256,256]{1,0:T(8,128)(2,1)S(1)}, bf16[256,256]{1,0:T(8,128)(2,1)}, u32[]{:S(2)}) copy-start(bf16[256,256]{1,0:T(8,128)(2,1)} %w_self.3) | copy-start | bytes 393220
  137.3 113.4 %all-to-all-start.2 = ((bf16[128,128,256]{2,1,0:T(8,128)(2,1)}), bf16[128,128,256]{2,1,0:T(8,128)(2,1)}, u32[]{:S(2)}, u32[]{:S(2)}) async-start(bf16[128,128,256]{2,1,0:T(8,128)(2,1)} %get-tuple-element.28), calls=%async_computation.2 | async-start | bytes 16777216 | tf_op jit(solution)/shard_map/all_to_all | solution.py:442
  146.0 1.6 copy-start.5
  147.6 1.6 copy-start.7
  149.2 101.6 %copy-start.1 = (f32[32,128,128]{2,1,0:T(8,128)S(1)}, f32[32,128,128]{2,1,0:T(8,128)}, u32[]{:S(2)}) copy-start(f32[32,128,128]{2,1,0:T(8,128)} %copy-done) | copy-start | bytes 6291460

commit v2 on v1

--- a/solution.py
+++ b/solution.py
@@ -16,6 +16,8 @@
 SEG = PER + 8
 PAIRS = 176
 GROUP = 8
+BATCH = 8
+BATCHES = NB // BATCH
 UNROLL = 4
 BF = jnp.bfloat16
 F32 = jnp.float32
@@ -42,7 +44,9 @@
     return lax.dot_general(a, b, (((1,), (1,)), ((), ())), preferred_element_type=F32)
 
 
-def pack_kernel(owner, slot, feat, out, rows, pos_v, pos_s, sem):
+def pack_kernel(owner, slot, feat, out, rows, held, pos_v, pos_s, sem, sem_feat):
+    load = pltpu.make_async_copy(feat, held, sem_feat)
+    load.start()
     sub = lax.broadcasted_iota(I32, (BLK, BLK), 0)
     lane = lax.broadcasted_iota(I32, (BLK, BLK), 1)
     before = jnp.concatenate([(sub < lane).astype(BF), jnp.ones((BLK, BLK), BF)], axis=1)
@@ -67,15 +71,14 @@
     copy.start()
     rows.reshape(ND, SEG, F)[:, PER:, :] = jnp.broadcast_to(digits[:, None, :], (ND, SEG - PER, F))
     copy.wait()
-
-    def move(i, _):
-        c = i >> 3
-        first = (i & 7) * 16
-        for u in range(16):
-            rows[pl.ds(pos_s[c, first + u], 1), :] = feat[pl.ds(i * 16 + u, 1), :]
-        return 0
-
-    lax.fori_loop(0, ROWS // 16, move, 0)
+    load.wait()
+
+    def move(c, _):
+        for u in range(BLK):
+            rows[pl.ds(pos_s[c, u], 1), :] = held[pl.ds(c * BLK + u, 1), :]
+        return 0
+
+    lax.fori_loop(0, ROWS // BLK, move, 0)
     out[...] = rows[...].reshape(ND, SEG, F).astype(BF)
 
 
@@ -83,15 +86,17 @@
     return pl.pallas_call(
         pack_kernel,
         out_shape=jax.ShapeDtypeStruct((ND, SEG, F), BF),
-        in_specs=[VMEM] * 3,
+        in_specs=[VMEM, VMEM, ANY],
         out_specs=VMEM,
         scratch_shapes=[
             pltpu.VMEM((ND * SEG, F), F32),
+            pltpu.VMEM((ROWS, F), F32),
             pltpu.VMEM((ROWS // BLK, BLK), I32),
             pltpu.SMEM((ROWS // BLK, BLK), I32),
             pltpu.SemaphoreType.DMA,
+            pltpu.SemaphoreType.DMA,
         ],
-        compiler_params=params(24),
+        compiler_params=params(56),
         name="pack",
     )(owner.reshape(ROWS // BLK, BLK), slot.reshape(ROWS // BLK, BLK), features)
 
@@ -99,17 +104,22 @@
 def unpack_kernel(send_blocks, arrived, relaid, send, rows, placed, slot_v, slot_s, sem, sem_out):
     rows[...] = arrived[...].astype(F32).reshape(ND * SEG, F)
     digits = rows[pl.ds(PER, ND, stride=SEG), :]
-    slot_v[...] = (digits * 64.0 + pltpu.roll(digits, F - PER, 1)).astype(I32)
+    slots = digits * 64.0 + pltpu.roll(digits, F - PER, 1)
+    lane = lax.broadcasted_iota(I32, (PER, F), 1)
+    slots = [jnp.where(lane < PER, slots[PER * g : PER * (g + 1)], 0.0) for g in range(ND // PER)]
+    slots = [slots[0]] + [pltpu.roll(slots[g], PER * g, 1) for g in range(1, ND // PER)]
+    slot_v[...] = sum(slots).astype(I32)
     copy = pltpu.make_async_copy(slot_v, slot_s, sem)
     copy.start()
     copy.wait()
 
     def move(i, _):
-        for u in range(PER):
-            placed[pl.ds(slot_s[i, u], 1), :] = rows[pl.ds(i * SEG + u, 1), :]
-        return 0
-
-    lax.fori_loop(0, ND, move, 0)
+        for u in range(F):
+            source = (i + PER * (u // PER)) * SEG + u % PER
+            placed[pl.ds(slot_s[i, u], 1), :] = rows[pl.ds(source, 1), :]
+        return 0
+
+    lax.fori_loop(0, PER, move, 0)
     relaid[...] = placed[...].reshape(NB, BLK, F).astype(BF)
 
     def post(d, _):
@@ -132,19 +142,19 @@
         scratch_shapes=[
             pltpu.VMEM((ND * SEG, F), F32),
             pltpu.VMEM((ROWS, F), F32),
-            pltpu.VMEM((ND, F), I32),
-            pltpu.SMEM((ND, F), I32),
+            pltpu.VMEM((PER, F), I32),
+            pltpu.SMEM((PER, F), I32),
             pltpu.SemaphoreType.DMA,
             pltpu.SemaphoreType.DMA,
         ],
-        compiler_params=params(24),
+        compiler_params=params(56),
         name="unpack",
     )(send_blocks, arrived)
 
 
 def prepare_kernel(
     row_s, col_s, count_s, send_blocks, tile_vals, relaid,
-    pairs, acc_out, inv_out, row_k, col_k, meta, dest, dest_at,
+    pairs, base, inv_out, row_k, col_k, meta, dest, dest_at,
     tiles, acc, held, cursor, tile_k, sem,
 ):
     load = pltpu.make_async_copy(tile_vals, tiles.at[pl.ds(0, TILES)], sem)
@@ -259,8 +269,9 @@
         return 0
 
     lax.fori_loop(n_own // UNROLL, n_all // UNROLL, far, 0)
-    acc_out[...] = acc[:, :, :BLK]
-    inv_out[...] = 1.0 / jnp.maximum(acc[:, :, BLK:], 1.0)
+    inv = 1.0 / jnp.maximum(acc[:, :, BLK:], 1.0)
+    inv_out[...] = inv
+    base[...] = acc[:, :, :BLK] * inv
 
 
 def prepare(tile_row, tile_col, tile_count, send_blocks, tile_vals, relaid):
@@ -287,14 +298,35 @@
             pltpu.SMEM((2 * PAIRS,), I32),
             pltpu.SemaphoreType.DMA,
         ],
-        compiler_params=params(48),
+        compiler_params=params(56),
         cost_estimate=cost(2 * 10**9, 32 * 2**20),
         name="prepare",
     )(tile_row, tile_col, tile_count, send_blocks, tile_vals, relaid)
 
 
-def add_pairs(first, last, start, held, sems, table, acc, row_k, col_k):
+def load_pairs(first, last, pairs, held, sems, begin=0, end=PAIRS):
     def group(c, _):
+        pltpu.make_async_copy(
+            pairs.at[pl.ds(first + c * GROUP, GROUP)], held.at[pl.ds(c * GROUP, GROUP)], sems.at[c]
+        ).start()
+        return 0
+
+    groups = (last - first) // GROUP
+    lax.fori_loop(jnp.minimum(begin, groups), jnp.minimum(end, groups), group, 0)
+
+
+def row_copies(i, base, inv, base_v, inv_v, sems_base, sems_inv):
+    b = pl.ds(BATCH * i, BATCH)
+    return (
+        pltpu.make_async_copy(base.at[b], base_v.at[b], sems_base.at[i]),
+        pltpu.make_async_copy(inv.at[b], inv_v.at[b], sems_inv.at[i]),
+    )
+
+
+def add_pairs(first, last, held, sems, table, acc, row_k, col_k, finish):
+    groups = (last - first) // GROUP
+
+    def group(c, done):
         pltpu.make_async_copy(held.at[pl.ds(0, GROUP)], held.at[pl.ds(0, GROUP)], sems.at[c]).wait()
         for u0 in range(0, GROUP, UNROLL):
             for u in range(u0, u0 + UNROLL):
@@ -302,140 +334,210 @@
                 x = jnp.concatenate([table[col_k[2 * k]], table[col_k[2 * k + 1]]], axis=0)
                 got = mm(held[c * GROUP + u], x)
                 acc[row_k[k]] += got
-        return 0
-
-    lax.fori_loop(0, (last - first) // GROUP, group, 0)
-
-
-def load_pairs(first, last, pairs, held, sems):
-    def group(c, _):
-        pltpu.make_async_copy(
-            pairs.at[pl.ds(first + c * GROUP, GROUP)], held.at[pl.ds(c * GROUP, GROUP)], sems.at[c]
-        ).start()
-        return 0
-
-    lax.fori_loop(0, (last - first) // GROUP, group, 0)
+        following = row_k[jnp.minimum(first + (c + 1) * GROUP, PAIRS - 1)]
+        upto = jnp.where(c + 1 < groups, following, NB) // BATCH
+        lax.fori_loop(done, upto, finish, 0)
+        return upto
+
+    lax.fori_loop(lax.fori_loop(0, groups, group, 0), BATCHES, finish, 0)
 
 
 def first_kernel(
-    row_k, col_k, meta, dest, dest_at, pairs, remote, relaid, acc_in, inv, w_self, w_neigh, w_next,
-    hidden, q_out, send,
-    held, acc, sems, sem_out,
+    row_k, col_k, meta, dest, dest_at, remote, pairs, base, inv, mean_out, send,
+    table, held, base_v, inv_v, acc, mean, sems, sems_base, sems_inv, sem_table, sem_mean, sem_out,
 ):
-    n_own = meta[0]
-    n_all = meta[1]
-    load_pairs(n_own, n_all, pairs, held, sems)
-    acc[...] = acc_in[...]
-    add_pairs(n_own, n_all, 0, held, sems, remote, acc, row_k, col_k)
-    weights = jnp.concatenate([w_self[...], w_neigh[...], w_neigh[...]], axis=0)
+    load_table = pltpu.make_async_copy(remote, table, sem_table)
+    rows = lambda i: row_copies(i, base, inv, base_v, inv_v, sems_base, sems_inv)
+
+    def load(i, _):
+        load_pairs(meta[0], meta[1], pairs, held, sems, 2 * i, 2 * i + 2)
+        for copy in rows(i):
+            copy.start()
+        return 0
+
+    load_table.start()
+    lax.fori_loop(0, EARLY, load, 0)
+    acc[...] = jnp.zeros_like(acc)
+    load_table.wait()
+    lax.fori_loop(EARLY, BATCHES, load, 0)
+    load_pairs(meta[0], meta[1], pairs, held, sems, 2 * BATCHES)
 
     def finish(i, _):
-        b = pl.ds(2 * i, 2)
-        mean = (acc[b] * inv[b]).reshape(2 * BLK, F)
-        high = mean.astype(BF)
-        low = (mean - high.astype(F32)).astype(BF)
-        x = jnp.concatenate([relaid[b].reshape(2 * BLK, F), high, low], axis=1)
-        h = jnp.maximum(mm(x, weights), 0.0).astype(BF)
-        hidden[b] = h.reshape(2, BLK, H)
-        q_out[b] = mm(h, w_next[...]).astype(BF).reshape(2, BLK, H)
-
-        def post(j, _):
-            d = dest[j]
-            blk = 2 * i + jnp.where(j >= dest_at[2 * i + 1], 1, 0)
-            pltpu.make_async_copy(q_out.at[blk], send.at[d], sem_out).start()
-            return 0
-
-        lax.fori_loop(dest_at[2 * i], dest_at[2 * i + 2], post, 0)
-        return 0
-
-    lax.fori_loop(0, NB // 2, finish, 0)
+        for copy in rows(i):
+            copy.wait()
+        b = pl.ds(BATCH * i, BATCH)
+        mean[b] = (base_v[b] + acc[b] * inv_v[b]).astype(BF)
+        pltpu.make_async_copy(mean.at[b], mean_out.at[b], sem_mean).start()
+
+        def post(j, blk):
+            blk = lax.while_loop(lambda at: j >= dest_at[at + 1], lambda at: at + 1, blk)
+            pltpu.make_async_copy(mean.at[blk], send.at[dest[j]], sem_out).start()
+            return blk
+
+        lax.fori_loop(dest_at[BATCH * i], dest_at[BATCH * (i + 1)], post, BATCH * i)
+        return 0
+
+    add_pairs(meta[0], meta[1], held, sems, table, acc, row_k, col_k, finish)
+    pltpu.make_async_copy(mean_out, mean_out, sem_mean).wait()
     pltpu.make_async_copy(send, send, sem_out).wait()
 
 
-def first(lists, pairs, remote, relaid, acc, inv, w_self, w_neigh, w_next):
+def first(lists, pairs, remote, base, inv):
     row_k, col_k, meta, dest, dest_at = lists
     return pl.pallas_call(
         first_kernel,
         out_shape=(
-            jax.ShapeDtypeStruct((NB, BLK, H), BF),
-            jax.ShapeDtypeStruct((NB, BLK, H), BF),
-            jax.ShapeDtypeStruct((ND, BLK, H), BF),
+            jax.ShapeDtypeStruct((NB, BLK, F), BF),
+            jax.ShapeDtypeStruct((ND, BLK, F), BF),
         ),
-        in_specs=[SMEM] * 5 + [ANY] + [VMEM] * 7,
-        out_specs=(VMEM, VMEM, ANY),
+        in_specs=[SMEM] * 5 + [ANY] * 4,
+        out_specs=(ANY, ANY),
         scratch_shapes=[
+            pltpu.VMEM((ND, BLK, F), BF),
             pltpu.VMEM((PAIRS, BLK, 2 * BLK), BF),
             pltpu.VMEM((NB, BLK, F), F32),
+            pltpu.VMEM((NB, BLK, BLK), F32),
+            pltpu.VMEM((NB, BLK, F), F32),
+            pltpu.VMEM((NB, BLK, F), BF),
             pltpu.SemaphoreType.DMA((PAIRS // GROUP,)),
-            pltpu.SemaphoreType.DMA,
-        ],
-        compiler_params=params(48),
+            pltpu.SemaphoreType.DMA((BATCHES,)),
+            pltpu.SemaphoreType.DMA((BATCHES,)),
+        ]
+        + [pltpu.SemaphoreType.DMA] * 3,
+        compiler_params=params(56),
         name="first_layer",
-    )(row_k, col_k, meta, dest, dest_at, pairs, remote, relaid, acc, inv, w_self, w_neigh, w_next)
-
-
-def own_kernel(row_k, col_k, meta, pairs, q, hidden, inv, w_self, base, held, acc, sems):
-    n_own = meta[0]
-    load_pairs(0, n_own, pairs, held, sems)
+    )(row_k, col_k, meta, dest, dest_at, remote, pairs, base, inv)
+
+
+def own_kernel(
+    row_k, col_k, meta, pairs, relaid, mean, inv, w_self1, w_neigh1, w_self2, w_neigh2, base,
+    hidden, acc, held, sems,
+):
+    load_pairs(0, meta[0], pairs, held, sems)
     acc[...] = jnp.zeros_like(acc)
-    add_pairs(0, n_own, 0, held, sems, q, acc, row_k, col_k)
-
-    def finish(b, _):
-        scale = inv[b]
-        base[b] = mm(hidden[b], w_self[...]) + acc[b] * jnp.concatenate([scale, scale], axis=1)
-        return 0
-
-    lax.fori_loop(0, NB, finish, 0)
-
-
-def own_part(lists, pairs, q, hidden, inv, w_self):
+    weights = jnp.concatenate([w_self1[...], w_neigh1[...]], axis=0)
+    final = jnp.concatenate([w_self2[...], w_neigh2[...], w_neigh2[...]], axis=0)
+
+    def layer(i, _):
+        b = pl.ds(2 * i, 2)
+        x = jnp.concatenate([relaid[b].reshape(2 * BLK, F), mean[b].reshape(2 * BLK, F)], axis=1)
+        hidden[b] = jnp.maximum(mm(x, weights), 0.0).astype(BF).reshape(2, BLK, H)
+        return 0
+
+    lax.fori_loop(0, NB // 2, layer, 0)
+
+    def finish(i, _):
+        b = pl.ds(BATCH * i, BATCH)
+        scale = inv[b].reshape(BATCH * BLK, BLK)
+        m = acc[b].reshape(BATCH * BLK, H) * jnp.concatenate([scale, scale], axis=1)
+        high = m.astype(BF)
+        low = (m - high.astype(F32)).astype(BF)
+        x = jnp.concatenate([hidden[b].reshape(BATCH * BLK, H), high, low], axis=1)
+        base[b] = mm(x, final).reshape(BATCH, BLK, H)
+        return 0
+
+    add_pairs(0, meta[0], held, sems, hidden, acc, row_k, col_k, finish)
+
+
+def own_part(lists, pairs, relaid, mean, inv, w_self1, w_neigh1, w_self2, w_neigh2):
     row_k, col_k, meta, _, _ = lists
     return pl.pallas_call(
         own_kernel,
         out_shape=jax.ShapeDtypeStruct((NB, BLK, H), F32),
-        in_specs=[SMEM] * 3 + [ANY] + [VMEM] * 4,
+        in_specs=[SMEM] * 3 + [ANY] + [VMEM] * 7,
         out_specs=VMEM,
         scratch_shapes=[
+            pltpu.VMEM((NB, BLK, H), BF),
+            pltpu.VMEM((NB, BLK, H), F32),
             pltpu.VMEM((PAIRS, BLK, 2 * BLK), BF),
-            pltpu.VMEM((NB, BLK, H), F32),
             pltpu.SemaphoreType.DMA((PAIRS // GROUP,)),
         ],
-        compiler_params=params(48),
+        compiler_params=params(56),
         cost_estimate=cost(2 * 10**9, 32 * 2**20),
         name="own_part",
-    )(row_k, col_k, meta, pairs, q, hidden, inv, w_self)
-
-
-def second_kernel(row_k, col_k, meta, pairs, remote, base, inv, out, held, acc, sems):
-    n_own = meta[0]
-    n_all = meta[1]
-    load_pairs(n_own, n_all, pairs, held, sems)
+    )(row_k, col_k, meta, pairs, relaid, mean, inv, w_self1, w_neigh1, w_self2, w_neigh2)
+
+
+EARLY = 2
+CHUNK = ND // BATCHES
+
+
+def second_kernel(
+    row_k, col_k, meta, near, far, pairs, base, inv, w_self1, w_neigh1, w_neigh2, out,
+    near_v, far_v, table, held, base_v, inv_v, acc, result,
+    sems, sems_near, sems_far, sems_base, sems_inv, sem_out,
+):
+    def chunk(c):
+        part = pl.ds(c * CHUNK, CHUNK)
+        return (
+            pltpu.make_async_copy(near.at[part], near_v.at[part], sems_near.at[c]),
+            pltpu.make_async_copy(far.at[part], far_v.at[part], sems_far.at[c]),
+        )
+
+    rows = lambda i: row_copies(i, base, inv, base_v, inv_v, sems_base, sems_inv)
+
+    def load(i):
+        load_pairs(meta[0], meta[1], pairs, held, sems, 2 * i, 2 * i + 2)
+        for copy in rows(i):
+            copy.start()
+
+    for c in range(ND // CHUNK):
+        for copy in chunk(c):
+            copy.start()
     acc[...] = jnp.zeros_like(acc)
-    add_pairs(n_own, n_all, 0, held, sems, remote, acc, row_k, col_k)
-
-    def finish(b, _):
-        scale = inv[b]
-        out[b] = (base[b] + acc[b] * jnp.concatenate([scale, scale], axis=1)).astype(BF)
-        return 0
-
-    lax.fori_loop(0, NB, finish, 0)
-
-
-def second(lists, pairs, remote, base, inv):
+    weights = jnp.concatenate([w_self1[...], w_neigh1[...]], axis=0)
+
+    def layer(c, _):
+        for copy in chunk(c):
+            copy.wait()
+        load(c)
+        for i in range(CHUNK // 2):
+            b = pl.ds(c * CHUNK + 2 * i, 2)
+            x = jnp.concatenate([near_v[b].reshape(2 * BLK, F), far_v[b].reshape(2 * BLK, F)], axis=1)
+            table[b] = jnp.maximum(mm(x, weights), 0.0).astype(BF).reshape(2, BLK, H)
+        return 0
+
+    lax.fori_loop(0, BATCHES, layer, 0)
+    load_pairs(meta[0], meta[1], pairs, held, sems, 2 * BATCHES)
+
+    def finish(i, _):
+        for copy in rows(i):
+            copy.wait()
+        b = pl.ds(BATCH * i, BATCH)
+        scale = inv_v[b].reshape(BATCH * BLK, BLK)
+        m = acc[b].reshape(BATCH * BLK, H) * jnp.concatenate([scale, scale], axis=1)
+        total = base_v[b].reshape(BATCH * BLK, H) + mm(m.astype(BF), w_neigh2[...])
+        result[b] = total.astype(BF).reshape(BATCH, BLK, H)
+        pltpu.make_async_copy(result.at[b], out.at[b], sem_out).start()
+        return 0
+
+    add_pairs(meta[0], meta[1], held, sems, table, acc, row_k, col_k, finish)
+    pltpu.make_async_copy(out, out, sem_out).wait()
+
+
+def second(lists, near, far, pairs, base, inv, w_self1, w_neigh1, w_neigh2):
     row_k, col_k, meta, _, _ = lists
     return pl.pallas_call(
         second_kernel,
         out_shape=jax.ShapeDtypeStruct((NB, BLK, H), BF),
-        in_specs=[SMEM] * 3 + [ANY] + [VMEM] * 3,
-        out_specs=VMEM,
+        in_specs=[SMEM] * 3 + [ANY] * 5 + [VMEM] * 3,
+        out_specs=ANY,
         scratch_shapes=[
+            pltpu.VMEM((ND, BLK, F), BF),
+            pltpu.VMEM((ND, BLK, F), BF),
+            pltpu.VMEM((ND, BLK, H), BF),
             pltpu.VMEM((PAIRS, BLK, 2 * BLK), BF),
             pltpu.VMEM((NB, BLK, H), F32),
+            pltpu.VMEM((NB, BLK, BLK), F32),
+            pltpu.VMEM((NB, BLK, H), F32),
+            pltpu.VMEM((NB, BLK, H), BF),
             pltpu.SemaphoreType.DMA((PAIRS // GROUP,)),
-        ],
-        compiler_params=params(48),
+        ]
+        + [pltpu.SemaphoreType.DMA((BATCHES,))] * 4
+        + [pltpu.SemaphoreType.DMA],
+        compiler_params=params(56),
         name="second_layer",
-    )(row_k, col_k, meta, pairs, remote, base, inv)
+    )(row_k, col_k, meta, near, far, pairs, base, inv, w_self1, w_neigh1, w_neigh2)
 
 
 def exchange(x):
@@ -449,12 +551,12 @@
     picks = send_blocks.reshape(ND)
     arrived = exchange(pack(features, owner, slot))
     relaid, send = unpack(picks, arrived)
-    remote = exchange(send)
-    pairs, acc, inv, *lists = prepare(tile_row, tile_col, tile_count, picks, tile_vals, relaid)
-    hidden, q, send = first(lists, pairs, remote, relaid, acc, inv, w_self1, w_neigh1, w_neigh2)
-    remote = exchange(send)
-    base = own_part(lists, pairs, q, hidden, inv, w_self2)
-    return second(lists, pairs, remote, base, inv).reshape(ROWS, H)
+    near = exchange(send)
+    pairs, base, inv, *lists = prepare(tile_row, tile_col, tile_count, picks, tile_vals, relaid)
+    mean, send = first(lists, pairs, near, base, inv)
+    far = exchange(send)
+    base = own_part(lists, pairs, relaid, mean, inv, w_self1, w_neigh1, w_self2, w_neigh2)
+    return second(lists, near, far, pairs, base, inv, w_self1, w_neigh1, w_neigh2).reshape(ROWS, H)
 
 
 def solution(mesh):

time: 263 us -> 186 us (0.71)
  the two profiles are of different devices: /device:TPU:19 before, /device:TPU:1 now
where the time goes in v2:
time: 186 us
  Pallas kernels  70 us (38%)
  waiting for transfers between devices  69.7 us (37%)
  blocking collectives  33.8 us (18%)
  starting transfers between devices  11.4 us (6%)
    all_to_all x2, waiting for transfers between devices, exchange(): return lax.all_to_all(x, 'dom', split_axis=0, concat_axis=0, tiled=True)  69.7 us
    all_to_all x1, blocking collectives, exchange(): return lax.all_to_all(x, 'dom', split_axis=0, concat_axis=0, tiled=True)  33.8 us
    pallas_call x1, Pallas kernels, prepare(): pl.pallas_call(prepare_kernel, out_shape=(jax.ShapeDtypeStruct((PAIRS, BL...  22.9 us
    pallas_call x1, Pallas kernels, own_part(): pl.pallas_call(own_kernel, out_shape=jax.ShapeDtypeStruct((NB, BLK, H), F...  12.2 us
    all_to_all x2, starting transfers between devices, exchange(): return lax.all_to_all(x, 'dom', split_axis=0, concat_axis=0, tiled=True)  11.4 us
    pallas_call x1, Pallas kernels, second(): pl.pallas_call(second_kernel, out_shape=jax.ShapeDtypeStruct((NB, BLK, H)...  10.1 us
    pallas_call x1, Pallas kernels, unpack(): pl.pallas_call(unpack_kernel, out_shape=(jax.ShapeDtypeStruct((NB, BLK, F...  8.83 us
    pallas_call x1, Pallas kernels, first(): pl.pallas_call(first_kernel, out_shape=(jax.ShapeDtypeStruct((NB, BLK, F)...  8.38 us
  transfers between devices with their start and end apart: 2, of which 2 were waited for; matrix products, arithmetic and copies ran while one was open for 0% of the time, Pallas kernels for 19%

profile of v2, /device:TPU:1, one launch (start us, length us, event | category | flops | bytes accessed | tf_op | source)
XLA Modules:
  0.0 185.6 jit_solution(1379224997423319736)
XLA Ops:
  0.0 7.6 %pack.1 = bf16[128,40,128]{2,1,0:T(8,128)(2,1)} custom-call(s32[32,128]{1,0:T(8,128)} %bitcast.4, s32[32,128]{1,0:T(8,128)} %bitcast.5, f32[4096,128]{1,0:T(8,128)} %feat.1), custom_call_target="tpu_custom_call" | custom-call | tf_op jit(solution)/shard_map/pack/pallas_call | solution.py:86
  7.7 33.8 %all_to_all.15.arrived = bf16[128,40,128]{2,1,0:T(8,128)(2,1)} all-to-all(bf16[128,40,128]{2,1,0:T(8,128)(2,1)} %pack.1), channel_id=1, replica_groups=mesh['dom'=128] {'dom'}, dimensions={0} | all-to-all | bytes 2621440 | tf_op jit(solution)/shard_map/all_to_all | solution.py:544
  41.4 8.8 %unpack.1 = (bf16[32,128,128]{2,1,0:T(8,128)(2,1)}, bf16[128,128,128]{2,1,0:T(8,128)(2,1)}) custom-call(s32[128]{0:T(128)} %bitcast.6, bf16[128,40,128]{2,1,0:T(8,128)(2,1)} %all_to_all.15.arrived), custom_call_target="tpu_custom_call" | custom-call | tf_op jit(solution)/shard_map/unpack/pallas_call | solution.py:134
  50.3 5.5 %all-to-all-start.1 = ((bf16[128,128,128]{2,1,0:T(8,128)(2,1)}), bf16[128,128,128]{2,1,0:T(8,128)(2,1)}, u32[]{:S(2)}, u32[]{:S(2)}) async-start(bf16[128,128,128]{2,1,0:T(8,128)(2,1)} %get-tuple-element.21), calls=%async_computation.1 | async-start | bytes 8388608 | tf_op jit(solution)/shard_map/all_to_all | solution.py:544
  56.4 22.9 %prepare.1 = (bf16[176,128,256]{2,1,0:T(8,128)(2,1)}, f32[32,128,128]{2,1,0:T(8,128)}, f32[32,128,128]{2,1,0:T(8,128)}, s32[176]{0:T(256)}, s32[352]{0:T(512)}, /*index=5*/s32[8]{0:T(128)}, s32[128]{0:T(128)}, s32[40]{0:T(128)}) custom-call(s32[256]{0:T(256)} %row_s.1, s32[256]{0:T(256)} %col_s.1, s32[1]{0:T(128)S(6)} %copy.13.count_s, s32[128]{0:T(128)} %bitcast.7, ...), custom_call_target="tpu_custom_call" | custom-call | flops 2000000000 | bytes 33554432 | tf_op jit(solution)/shard_map/prepare/pallas_call | solution.py:279
  79.3 29.2 %all-to-all-done.1.remote.near = bf16[128,128,128]{2,1,0:T(8,128)(2,1)} async-done(((bf16[128,128,128]{2,1,0:T(8,128)(2,1)}), bf16[128,128,128]{2,1,0:T(8,128)(2,1)}, u32[]{:S(2)}, u32[]{:S(2)}) %all-to-all-start.1) | async-done | bytes 4194336 | tf_op jit(solution)/shard_map/all_to_all | solution.py:544
  108.5 8.4 %first_layer.1 = (bf16[32,128,128]{2,1,0:T(8,128)(2,1)}, bf16[128,128,128]{2,1,0:T(8,128)(2,1)}) custom-call(s32[176]{0:T(256)} %get-tuple-element.18.row_k, s32[352]{0:T(512)} %get-tuple-element.19.col_k, s32[8]{0:T(128)} %get-tuple-element.20.meta, s32[128]{0:T(128)} %get-tuple-element.22.dest, s32[40]{0:T(128)} %get-tuple-element.23.dest_at, ...), custom_call_target="tpu_custom_call" | custom-call | tf_op jit(solution)/shard_map/first_layer/pallas_call | solution.py:387
  116.9 5.9 %all-to-all-start.2 = ((bf16[128,128,128]{2,1,0:T(8,128)(2,1)}), bf16[128,128,128]{2,1,0:T(8,128)(2,1)}, u32[]{:S(2)}, u32[]{:S(2)}) async-start(bf16[128,128,128]{2,1,0:T(8,128)(2,1)} %get-tuple-element.27), calls=%async_computation.2 | async-start | bytes 8388608 | tf_op jit(solution)/shard_map/all_to_all | solution.py:544
  122.8 12.2 %own_part.1.base = f32[32,128,256]{2,1,0:T(8,128)} custom-call(s32[176]{0:T(256)} %get-tuple-element.18.row_k, s32[352]{0:T(512)} %get-tuple-element.19.col_k, s32[8]{0:T(128)} %get-tuple-element.20.meta, bf16[176,128,256]{2,1,0:T(8,128)(2,1)} %get-tuple-element.24.pairs, bf16[32,128,128]{2,1,0:T(8,128)(2,1)} %get-tuple-element.17.relaid, ...), custom_call_target="tpu_custom_call" | custom-call | flops 2000000000 | bytes 33554432 | tf_op jit(solution)/shard_map/own_part/pallas_call | solution.py:444
  135.0 40.5 %all-to-all-done.2.far = bf16[128,128,128]{2,1,0:T(8,128)(2,1)} async-done(((bf16[128,128,128]{2,1,0:T(8,128)(2,1)}), bf16[128,128,128]{2,1,0:T(8,128)(2,1)}, u32[]{:S(2)}, u32[]{:S(2)}) %all-to-all-start.2) | async-done | bytes 4194336 | tf_op jit(solution)/shard_map/all_to_all | solution.py:544
  175.5 10.1 %second_layer.1 = bf16[32,128,256]{2,1,0:T(8,128)(2,1)} custom-call(s32[176]{0:T(256)} %get-tuple-element.18.row_k, s32[352]{0:T(512)} %get-tuple-element.19.col_k, s32[8]{0:T(128)} %get-tuple-element.20.meta, bf16[128,128,128]{2,1,0:T(8,128)(2,1)} %all-to-all-done.1.remote.near, bf16[128,128,128]{2,1,0:T(8,128)(2,1)} %all-to-all-done.2.far, ...), custom_call_target="tpu_custom_call" | custom-call | tf_op jit(solution)/shard_map/second_layer/pallas_call | solution.py:520
Async XLA Ops:
  50.3 58.2 %all-to-all-start.1 = ((bf16[128,128,128]{2,1,0:T(8,128)(2,1)}), bf16[128,128,128]{2,1,0:T(8,128)(2,1)}, u32[]{:S(2)}, u32[]{:S(2)}) async-start(bf16[128,128,128]{2,1,0:T(8,128)(2,1)} %get-tuple-element.21), calls=%async_computation.1 | async-start | bytes 8388608 | tf_op jit(solution)/shard_map/all_to_all | solution.py:544
  116.9 58.6 %all-to-all-start.2 = ((bf16[128,128,128]{2,1,0:T(8,128)(2,1)}), bf16[128,128,128]{2,1,0:T(8,128)(2,1)}, u32[]{:S(2)}, u32[]{:S(2)}) async-start(bf16[128,128,128]{2,1,0:T(8,128)(2,1)} %get-tuple-element.27), calls=%async_computation.2 | async-start | bytes 8388608 | tf_op jit(solution)/shard_map/all_to_all | solution.py:544

commit v3 on v2

--- a/solution.py
+++ b/solution.py
@@ -14,11 +14,12 @@
 ND = 128
 PER = ROWS // ND
 SEG = PER + 8
-PAIRS = 176
-GROUP = 8
+PAIRS = 192
+GROUP = 16
 BATCH = 8
 BATCHES = NB // BATCH
 UNROLL = 4
+ROW, COL, META, DEST, DEST_AT, LISTS = 0, PAIRS, 3 * PAIRS, 3 * PAIRS + 8, 3 * PAIRS + 136, 1024
 BF = jnp.bfloat16
 F32 = jnp.float32
 I32 = jnp.int32
@@ -44,14 +45,20 @@
     return lax.dot_general(a, b, (((1,), (1,)), ((), ())), preferred_element_type=F32)
 
 
-def pack_kernel(owner, slot, feat, out, rows, held, pos_v, pos_s, sem, sem_feat):
+def pack_kernel(owner_in, slot_in, feat, out, rows, held, owner, slot, pos_v, pos_s, sem, sem_feat, sem_owner, sem_slot):
+    load_owner = pltpu.make_async_copy(owner_in, owner, sem_owner)
+    load_slot = pltpu.make_async_copy(slot_in, slot, sem_slot)
     load = pltpu.make_async_copy(feat, held, sem_feat)
+    load_owner.start()
+    load_slot.start()
     load.start()
     sub = lax.broadcasted_iota(I32, (BLK, BLK), 0)
     lane = lax.broadcasted_iota(I32, (BLK, BLK), 1)
     before = jnp.concatenate([(sub < lane).astype(BF), jnp.ones((BLK, BLK), BF)], axis=1)
     carry = jnp.zeros((BLK, BLK), F32)
     digits = jnp.zeros((BLK, BLK), F32)
+    load_owner.wait()
+    load_slot.wait()
     for c in range(ROWS // BLK):
         own = owner[c : c + 1, :]
         hit = own == sub
@@ -86,23 +93,39 @@
     return pl.pallas_call(
         pack_kernel,
         out_shape=jax.ShapeDtypeStruct((ND, SEG, F), BF),
-        in_specs=[VMEM, VMEM, ANY],
+        in_specs=[ANY] * 3,
         out_specs=VMEM,
         scratch_shapes=[
             pltpu.VMEM((ND * SEG, F), F32),
             pltpu.VMEM((ROWS, F), F32),
             pltpu.VMEM((ROWS // BLK, BLK), I32),
+            pltpu.VMEM((ROWS // BLK, BLK), I32),
+            pltpu.VMEM((ROWS // BLK, BLK), I32),
             pltpu.SMEM((ROWS // BLK, BLK), I32),
-            pltpu.SemaphoreType.DMA,
-            pltpu.SemaphoreType.DMA,
-        ],
+        ]
+        + [pltpu.SemaphoreType.DMA] * 4,
         compiler_params=params(56),
         name="pack",
     )(owner.reshape(ROWS // BLK, BLK), slot.reshape(ROWS // BLK, BLK), features)
 
 
-def unpack_kernel(send_blocks, arrived, relaid, send, rows, placed, slot_v, slot_s, sem, sem_out):
-    rows[...] = arrived[...].astype(F32).reshape(ND * SEG, F)
+PARTS = 4
+
+
+def unpack_kernel(
+    send_in, arrived, relaid_out, send,
+    send_blocks, held, rows, placed, relaid, slot_v, slot_s, sem, sem_send, sems, sem_relaid, sem_out,
+):
+    part = lambda i: pl.ds(i * (ND // PARTS), ND // PARTS)
+    loads = [pltpu.make_async_copy(arrived.at[part(i)], held.at[part(i)], sems.at[i]) for i in range(PARTS)]
+    load_send = pltpu.make_async_copy(send_in, send_blocks, sem_send)
+    for load in loads:
+        load.start()
+    load_send.start()
+    for i, load in enumerate(loads):
+        load.wait()
+        size = ND // PARTS * SEG
+        rows[pl.ds(i * size, size), :] = held[part(i)].astype(F32).reshape(size, F)
     digits = rows[pl.ds(PER, ND, stride=SEG), :]
     slots = digits * 64.0 + pltpu.roll(digits, F - PER, 1)
     lane = lax.broadcasted_iota(I32, (PER, F), 1)
@@ -121,13 +144,17 @@
 
     lax.fori_loop(0, PER, move, 0)
     relaid[...] = placed[...].reshape(NB, BLK, F).astype(BF)
+    load_send.wait()
 
     def post(d, _):
         pltpu.make_async_copy(relaid.at[send_blocks[d]], send.at[d], sem_out).start()
         return 0
 
     lax.fori_loop(0, ND, post, 0)
+    keep = pltpu.make_async_copy(relaid, relaid_out, sem_relaid)
+    keep.start()
     pltpu.make_async_copy(send, send, sem_out).wait()
+    keep.wait()
 
 
 def unpack(send_blocks, arrived):
@@ -137,13 +164,19 @@
             jax.ShapeDtypeStruct((NB, BLK, F), BF),
             jax.ShapeDtypeStruct((ND, BLK, F), BF),
         ),
-        in_specs=[SMEM, VMEM],
-        out_specs=(VMEM, ANY),
+        in_specs=[ANY, ANY],
+        out_specs=(ANY, ANY),
         scratch_shapes=[
+            pltpu.SMEM((ND,), I32),
+            pltpu.VMEM((ND, SEG, F), BF),
             pltpu.VMEM((ND * SEG, F), F32),
             pltpu.VMEM((ROWS, F), F32),
+            pltpu.VMEM((NB, BLK, F), BF),
             pltpu.VMEM((PER, F), I32),
             pltpu.SMEM((PER, F), I32),
+            pltpu.SemaphoreType.DMA,
+            pltpu.SemaphoreType.DMA,
+            pltpu.SemaphoreType.DMA((PARTS,)),
             pltpu.SemaphoreType.DMA,
             pltpu.SemaphoreType.DMA,
         ],
@@ -154,7 +187,7 @@
 
 def prepare_kernel(
     row_s, col_s, count_s, send_blocks, tile_vals, relaid,
-    pairs, base, inv_out, row_k, col_k, meta, dest, dest_at,
+    pairs, base, inv_out, lists,
     tiles, acc, held, cursor, tile_k, sem,
 ):
     load = pltpu.make_async_copy(tile_vals, tiles.at[pl.ds(0, TILES)], sem)
@@ -169,10 +202,10 @@
     lax.fori_loop(0, 2 * NB, clear, 0)
 
     def clear_pair(i, _):
-        row_k[i] = 0
+        lists[ROW + i] = 0
         for s in (0, 1):
             tile_k[2 * i + s] = TILES
-            col_k[2 * i + s] = 0
+            lists[COL + 2 * i + s] = 0
         return 0
 
     lax.fori_loop(0, PAIRS, clear_pair, 0)
@@ -194,8 +227,8 @@
     n_own = (n_own + GROUP - 1) // GROUP * GROUP
     n_all = lax.fori_loop(NB, 2 * NB, starts, n_own)
     n_all = (n_all + GROUP - 1) // GROUP * GROUP
-    meta[0] = n_own
-    meta[1] = n_all
+    lists[META + 0] = n_own
+    lists[META + 1] = n_all
 
     def place(t, _):
         row = row_s[t]
@@ -206,8 +239,8 @@
         at = cursor[g]
         cursor[g] = at + 1
         tile_k[at] = t
-        col_k[at] = col
-        row_k[at >> 1] = row
+        lists[COL + at] = col
+        lists[ROW + at >> 1] = row
         return 0
 
     lax.fori_loop(0, used, place, 0)
@@ -228,16 +261,16 @@
     def starts_dest(b, at):
         n = cursor[b]
         cursor[b] = at
-        dest_at[b] = at
+        lists[DEST_AT + b] = at
         return at + n
 
-    dest_at[NB] = lax.fori_loop(0, NB, starts_dest, 0)
+    lists[DEST_AT + NB] = lax.fori_loop(0, NB, starts_dest, 0)
 
     def place_dest(d, _):
         b = send_blocks[d]
         at = cursor[b]
         cursor[b] = at + 1
-        dest[at] = d
+        lists[DEST + at] = d
         return 0
 
     lax.fori_loop(0, ND, place_dest, 0)
@@ -254,9 +287,9 @@
         for u in range(UNROLL):
             k = i * UNROLL + u
             v = fetch(k)
-            x = jnp.concatenate([relaid[col_k[2 * k]], relaid[col_k[2 * k + 1]]], axis=0)
+            x = jnp.concatenate([relaid[lists[COL + 2 * k]], relaid[lists[COL + 2 * k + 1]]], axis=0)
             got = mm(v, jnp.concatenate([x, ones], axis=1))
-            acc[row_k[k]] += got
+            acc[lists[ROW + k]] += got
         return 0
 
     lax.fori_loop(0, n_own // UNROLL, own, 0)
@@ -264,7 +297,7 @@
     def far(i, _):
         for u in range(UNROLL):
             k = i * UNROLL + u
-            r = row_k[k]
+            r = lists[ROW + k]
             acc[r, :, BLK:] += mm(fetch(k), ones)
         return 0
 
@@ -275,21 +308,16 @@
 
 
 def prepare(tile_row, tile_col, tile_count, send_blocks, tile_vals, relaid):
-    ints = lambda n: jax.ShapeDtypeStruct((n,), I32)
     return pl.pallas_call(
         prepare_kernel,
         out_shape=(
             jax.ShapeDtypeStruct((PAIRS, BLK, 2 * BLK), BF),
             jax.ShapeDtypeStruct((NB, BLK, F), F32),
             jax.ShapeDtypeStruct((NB, BLK, BLK), F32),
-            ints(PAIRS),
-            ints(2 * PAIRS),
-            ints(8),
-            ints(ND),
-            ints(NB + 8),
+            jax.ShapeDtypeStruct((LISTS,), I32),
         ),
         in_specs=[SMEM, SMEM, SMEM, SMEM, ANY, VMEM],
-        out_specs=(VMEM, VMEM, VMEM, SMEM, SMEM, SMEM, SMEM, SMEM),
+        out_specs=(VMEM, VMEM, VMEM, SMEM),
         scratch_shapes=[
             pltpu.VMEM((TILES + 1, BLK, BLK), I32),
             pltpu.VMEM((NB, BLK, 2 * BLK), F32),
@@ -323,7 +351,7 @@
     )
 
 
-def add_pairs(first, last, held, sems, table, acc, row_k, col_k, finish):
+def add_pairs(first, last, held, sems, table, acc, lists, finish):
     groups = (last - first) // GROUP
 
     def group(c, done):
@@ -331,10 +359,10 @@
         for u0 in range(0, GROUP, UNROLL):
             for u in range(u0, u0 + UNROLL):
                 k = first + c * GROUP + u
-                x = jnp.concatenate([table[col_k[2 * k]], table[col_k[2 * k + 1]]], axis=0)
+                x = jnp.concatenate([table[lists[COL + 2 * k]], table[lists[COL + 2 * k + 1]]], axis=0)
                 got = mm(held[c * GROUP + u], x)
-                acc[row_k[k]] += got
-        following = row_k[jnp.minimum(first + (c + 1) * GROUP, PAIRS - 1)]
+                acc[lists[ROW + k]] += got
+        following = lists[ROW + jnp.minimum(first + (c + 1) * GROUP, PAIRS - 1)]
         upto = jnp.where(c + 1 < groups, following, NB) // BATCH
         lax.fori_loop(done, upto, finish, 0)
         return upto
@@ -343,24 +371,27 @@
 
 
 def first_kernel(
-    row_k, col_k, meta, dest, dest_at, remote, pairs, base, inv, mean_out, send,
-    table, held, base_v, inv_v, acc, mean, sems, sems_base, sems_inv, sem_table, sem_mean, sem_out,
+    lists_in, remote, pairs, base, inv, mean_out, send,
+    lists, table, held, base_v, inv_v, acc, mean, sems, sems_base, sems_inv, sem_lists, sem_table, sem_mean, sem_out,
 ):
     load_table = pltpu.make_async_copy(remote, table, sem_table)
     rows = lambda i: row_copies(i, base, inv, base_v, inv_v, sems_base, sems_inv)
 
     def load(i, _):
-        load_pairs(meta[0], meta[1], pairs, held, sems, 2 * i, 2 * i + 2)
+        load_pairs(lists[META + 0], lists[META + 1], pairs, held, sems, LOADS * i, LOADS * (i + 1))
         for copy in rows(i):
             copy.start()
         return 0
 
+    load_lists = pltpu.make_async_copy(lists_in, lists, sem_lists)
+    load_lists.start()
     load_table.start()
+    load_lists.wait()
     lax.fori_loop(0, EARLY, load, 0)
     acc[...] = jnp.zeros_like(acc)
     load_table.wait()
     lax.fori_loop(EARLY, BATCHES, load, 0)
-    load_pairs(meta[0], meta[1], pairs, held, sems, 2 * BATCHES)
+    load_pairs(lists[META + 0], lists[META + 1], pairs, held, sems, LOADS * BATCHES)
 
     def finish(i, _):
         for copy in rows(i):
@@ -370,29 +401,29 @@
         pltpu.make_async_copy(mean.at[b], mean_out.at[b], sem_mean).start()
 
         def post(j, blk):
-            blk = lax.while_loop(lambda at: j >= dest_at[at + 1], lambda at: at + 1, blk)
-            pltpu.make_async_copy(mean.at[blk], send.at[dest[j]], sem_out).start()
+            blk = lax.while_loop(lambda at: j >= lists[DEST_AT + at + 1], lambda at: at + 1, blk)
+            pltpu.make_async_copy(mean.at[blk], send.at[lists[DEST + j]], sem_out).start()
             return blk
 
-        lax.fori_loop(dest_at[BATCH * i], dest_at[BATCH * (i + 1)], post, BATCH * i)
-        return 0
-
-    add_pairs(meta[0], meta[1], held, sems, table, acc, row_k, col_k, finish)
+        lax.fori_loop(lists[DEST_AT + BATCH * i], lists[DEST_AT + BATCH * (i + 1)], post, BATCH * i)
+        return 0
+
+    add_pairs(lists[META + 0], lists[META + 1], held, sems, table, acc, lists, finish)
     pltpu.make_async_copy(mean_out, mean_out, sem_mean).wait()
     pltpu.make_async_copy(send, send, sem_out).wait()
 
 
 def first(lists, pairs, remote, base, inv):
-    row_k, col_k, meta, dest, dest_at = lists
     return pl.pallas_call(
         first_kernel,
         out_shape=(
             jax.ShapeDtypeStruct((NB, BLK, F), BF),
             jax.ShapeDtypeStruct((ND, BLK, F), BF),
         ),
-        in_specs=[SMEM] * 5 + [ANY] * 4,
+        in_specs=[ANY] * 5,
         out_specs=(ANY, ANY),
         scratch_shapes=[
+            pltpu.SMEM((LISTS,), I32),
             pltpu.VMEM((ND, BLK, F), BF),
             pltpu.VMEM((PAIRS, BLK, 2 * BLK), BF),
             pltpu.VMEM((NB, BLK, F), F32),
@@ -403,17 +434,17 @@
             pltpu.SemaphoreType.DMA((BATCHES,)),
             pltpu.SemaphoreType.DMA((BATCHES,)),
         ]
-        + [pltpu.SemaphoreType.DMA] * 3,
+        + [pltpu.SemaphoreType.DMA] * 4,
         compiler_params=params(56),
         name="first_layer",
-    )(row_k, col_k, meta, dest, dest_at, remote, pairs, base, inv)
+    )(lists, remote, pairs, base, inv)
 
 
 def own_kernel(
-    row_k, col_k, meta, pairs, relaid, mean, inv, w_self1, w_neigh1, w_self2, w_neigh2, base,
+    lists, pairs, relaid, mean, inv, w_self1, w_neigh1, w_self2, w_neigh2, base,
     hidden, acc, held, sems,
 ):
-    load_pairs(0, meta[0], pairs, held, sems)
+    load_pairs(0, lists[META + 0], pairs, held, sems)
     acc[...] = jnp.zeros_like(acc)
     weights = jnp.concatenate([w_self1[...], w_neigh1[...]], axis=0)
     final = jnp.concatenate([w_self2[...], w_neigh2[...], w_neigh2[...]], axis=0)
@@ -436,15 +467,14 @@
         base[b] = mm(x, final).reshape(BATCH, BLK, H)
         return 0
 
-    add_pairs(0, meta[0], held, sems, hidden, acc, row_k, col_k, finish)
+    add_pairs(0, lists[META + 0], held, sems, hidden, acc, lists, finish)
 
 
 def own_part(lists, pairs, relaid, mean, inv, w_self1, w_neigh1, w_self2, w_neigh2):
-    row_k, col_k, meta, _, _ = lists
     return pl.pallas_call(
         own_kernel,
         out_shape=jax.ShapeDtypeStruct((NB, BLK, H), F32),
-        in_specs=[SMEM] * 3 + [ANY] + [VMEM] * 7,
+        in_specs=[SMEM, ANY] + [VMEM] * 7,
         out_specs=VMEM,
         scratch_shapes=[
             pltpu.VMEM((NB, BLK, H), BF),
@@ -455,15 +485,16 @@
         compiler_params=params(56),
         cost_estimate=cost(2 * 10**9, 32 * 2**20),
         name="own_part",
-    )(row_k, col_k, meta, pairs, relaid, mean, inv, w_self1, w_neigh1, w_self2, w_neigh2)
+    )(lists, pairs, relaid, mean, inv, w_self1, w_neigh1, w_self2, w_neigh2)
 
 
 EARLY = 2
+LOADS = 2
 CHUNK = ND // BATCHES
 
 
 def second_kernel(
-    row_k, col_k, meta, near, far, pairs, base, inv, w_self1, w_neigh1, w_neigh2, out,
+    lists, near, far, pairs, base, inv, w_self1, w_neigh1, w_neigh2, out,
     near_v, far_v, table, held, base_v, inv_v, acc, result,
     sems, sems_near, sems_far, sems_base, sems_inv, sem_out,
 ):
@@ -477,7 +508,7 @@
     rows = lambda i: row_copies(i, base, inv, base_v, inv_v, sems_base, sems_inv)
 
     def load(i):
-        load_pairs(meta[0], meta[1], pairs, held, sems, 2 * i, 2 * i + 2)
+        load_pairs(lists[META + 0], lists[META + 1], pairs, held, sems, LOADS * i, LOADS * (i + 1))
         for copy in rows(i):
             copy.start()
 
@@ -498,7 +529,7 @@
         return 0
 
     lax.fori_loop(0, BATCHES, layer, 0)
-    load_pairs(meta[0], meta[1], pairs, held, sems, 2 * BATCHES)
+    load_pairs(lists[META + 0], lists[META + 1], pairs, held, sems, LOADS * BATCHES)
 
     def finish(i, _):
         for copy in rows(i):
@@ -511,16 +542,15 @@
         pltpu.make_async_copy(result.at[b], out.at[b], sem_out).start()
         return 0
 
-    add_pairs(meta[0], meta[1], held, sems, table, acc, row_k, col_k, finish)
+    add_pairs(lists[META + 0], lists[META + 1], held, sems, table, acc, lists, finish)
     pltpu.make_async_copy(out, out, sem_out).wait()
 
 
 def second(lists, near, far, pairs, base, inv, w_self1, w_neigh1, w_neigh2):
-    row_k, col_k, meta, _, _ = lists
     return pl.pallas_call(
         second_kernel,
         out_shape=jax.ShapeDtypeStruct((NB, BLK, H), BF),
-        in_specs=[SMEM] * 3 + [ANY] * 5 + [VMEM] * 3,
+        in_specs=[SMEM] + [ANY] * 5 + [VMEM] * 3,
         out_specs=ANY,
         scratch_shapes=[
             pltpu.VMEM((ND, BLK, F), BF),
@@ -537,7 +567,7 @@
         + [pltpu.SemaphoreType.DMA],
         compiler_params=params(56),
         name="second_layer",
-    )(row_k, col_k, meta, near, far, pairs, base, inv, w_self1, w_neigh1, w_neigh2)
+    )(lists, near, far, pairs, base, inv, w_self1, w_neigh1, w_neigh2)
 
 
 def exchange(x):
@@ -552,7 +582,7 @@
     arrived = exchange(pack(features, owner, slot))
     relaid, send = unpack(picks, arrived)
     near = exchange(send)
-    pairs, base, inv, *lists = prepare(tile_row, tile_col, tile_count, picks, tile_vals, relaid)
+    pairs, base, inv, lists = prepare(tile_row, tile_col, tile_count, picks, tile_vals, relaid)
     mean, send = first(lists, pairs, near, base, inv)
     far = exchange(send)
     base = own_part(lists, pairs, relaid, mean, inv, w_self1, w_neigh1, w_self2, w_neigh2)

time: 186 us -> 185 us (level)
  Pallas kernels: 70 us -> 74.2 us
  waiting for transfers between devices: 69.7 us -> 65.7 us
    pallas_call x1, Pallas kernels: 22.9 us -> 27.5 us  [prepare(): pl.pallas_call(prepare_kernel, out_shape=(jax.ShapeDtypeStruct((PAIRS, BL...]
    all_to_all x2, waiting for transfers between devices: 69.7 us -> 65.7 us  [exchange(): return lax.all_to_all(x, 'dom', split_axis=0, concat_axis=0, tiled=True)]
  transfers between devices with their start and end apart: 2 -> 2, of which waited for: 2 -> 2; matrix products, arithmetic and copies ran while one was open for 0% -> 0% of each run, Pallas kernels for 19% -> 21%
where the time goes in v3:
time: 185 us
  Pallas kernels  74.2 us (40%)
  waiting for transfers between devices  65.7 us (36%)
  blocking collectives  33.8 us (18%)
  starting transfers between devices  10.4 us (6%)
    all_to_all x2, waiting for transfers between devices, exchange(): return lax.all_to_all(x, 'dom', split_axis=0, concat_axis=0, tiled=True)  65.7 us
    all_to_all x1, blocking collectives, exchange(): return lax.all_to_all(x, 'dom', split_axis=0, concat_axis=0, tiled=True)  33.8 us
    pallas_call x1, Pallas kernels, prepare(): pl.pallas_call(prepare_kernel, out_shape=(jax.ShapeDtypeStruct((PAIRS, BL...  27.5 us
    pallas_call x1, Pallas kernels, own_part(): pl.pallas_call(own_kernel, out_shape=jax.ShapeDtypeStruct((NB, BLK, H), F...  11.6 us
    pallas_call x1, Pallas kernels, second(): pl.pallas_call(second_kernel, out_shape=jax.ShapeDtypeStruct((NB, BLK, H)...  10.7 us
    all_to_all x2, starting transfers between devices, exchange(): return lax.all_to_all(x, 'dom', split_axis=0, concat_axis=0, tiled=True)  10.4 us
    pallas_call x1, Pallas kernels, first(): pl.pallas_call(first_kernel, out_shape=(jax.ShapeDtypeStruct((NB, BLK, F)...  8.52 us
    pallas_call x1, Pallas kernels, unpack(): pl.pallas_call(unpack_kernel, out_shape=(jax.ShapeDtypeStruct((NB, BLK, F...  8.14 us
  transfers between devices with their start and end apart: 2, of which 2 were waited for; matrix products, arithmetic and copies ran while one was open for 0% of the time, Pallas kernels for 21%

profile of v3, /device:TPU:1, one launch (start us, length us, event | category | flops | bytes accessed | tf_op | source)
XLA Modules:
  0.0 184.7 jit_solution(11887469049481475814)
XLA Ops:
  0.0 7.7 %pack.1 = bf16[128,40,128]{2,1,0:T(8,128)(2,1)} custom-call(s32[32,128]{1,0:T(8,128)} %bitcast.4, s32[32,128]{1,0:T(8,128)} %bitcast.5, f32[4096,128]{1,0:T(8,128)} %feat.1), custom_call_target="tpu_custom_call" | custom-call | tf_op jit(solution)/shard_map/pack/pallas_call | solution.py:93
  7.7 33.8 %all_to_all.15.arrived = bf16[128,40,128]{2,1,0:T(8,128)(2,1)} all-to-all(bf16[128,40,128]{2,1,0:T(8,128)(2,1)} %pack.1), channel_id=1, replica_groups=mesh['dom'=128] {'dom'}, dimensions={0} | all-to-all | bytes 2621440 | tf_op jit(solution)/shard_map/all_to_all | solution.py:574
  41.5 8.1 %unpack.1 = (bf16[32,128,128]{2,1,0:T(8,128)(2,1)}, bf16[128,128,128]{2,1,0:T(8,128)(2,1)}) custom-call(s32[128]{0:T(128)} %bitcast.6, bf16[128,40,128]{2,1,0:T(8,128)(2,1)} %all_to_all.15.arrived), custom_call_target="tpu_custom_call" | custom-call | tf_op jit(solution)/shard_map/unpack/pallas_call | solution.py:161
  49.6 5.4 %all-to-all-start.1 = ((bf16[128,128,128]{2,1,0:T(8,128)(2,1)}), bf16[128,128,128]{2,1,0:T(8,128)(2,1)}, u32[]{:S(2)}, u32[]{:S(2)}) async-start(bf16[128,128,128]{2,1,0:T(8,128)(2,1)} %get-tuple-element.15), calls=%async_computation.1 | async-start | bytes 8388608 | tf_op jit(solution)/shard_map/all_to_all | solution.py:574
  55.7 27.5 %prepare.1 = (bf16[192,128,256]{2,1,0:T(8,128)(2,1)}, f32[32,128,128]{2,1,0:T(8,128)}, f32[32,128,128]{2,1,0:T(8,128)}, s32[1024]{0:T(1024)}) custom-call(s32[256]{0:T(256)} %row_s.1, s32[256]{0:T(256)} %col_s.1, s32[1]{0:T(128)S(6)} %copy.13.count_s, s32[128]{0:T(128)} %bitcast.7, s32[256,128,128]{2,1,0:T(8,128)} %tile_vals.1, ...), custom_call_target="tpu_custom_call" | custom-call | flops 2000000000 | bytes 33554432 | tf_op jit(solution)/shard_map/prepare/pallas_call | solution.py:311
  83.2 24.7 %all-to-all-done.1.remote.near = bf16[128,128,128]{2,1,0:T(8,128)(2,1)} async-done(((bf16[128,128,128]{2,1,0:T(8,128)(2,1)}), bf16[128,128,128]{2,1,0:T(8,128)(2,1)}, u32[]{:S(2)}, u32[]{:S(2)}) %all-to-all-start.1) | async-done | bytes 4194336 | tf_op jit(solution)/shard_map/all_to_all | solution.py:574
  107.8 8.5 %first_layer.1 = (bf16[32,128,128]{2,1,0:T(8,128)(2,1)}, bf16[128,128,128]{2,1,0:T(8,128)(2,1)}) custom-call(s32[1024]{0:T(1024)} %get-tuple-element.14.lists_in.lists, bf16[128,128,128]{2,1,0:T(8,128)(2,1)} %all-to-all-done.1.remote.near, bf16[192,128,256]{2,1,0:T(8,128)(2,1)} %get-tuple-element.16.pairs, f32[32,128,128]{2,1,0:T(8,128)} %get-tuple-element.17.base, ...), custom_call_target="tpu_custom_call" | custom-call | tf_op jit(solution)/shard_map/first_layer/pallas_call | solution.py:417
  116.4 4.9 %all-to-all-start.2 = ((bf16[128,128,128]{2,1,0:T(8,128)(2,1)}), bf16[128,128,128]{2,1,0:T(8,128)(2,1)}, u32[]{:S(2)}, u32[]{:S(2)}) async-start(bf16[128,128,128]{2,1,0:T(8,128)(2,1)} %get-tuple-element.19), calls=%async_computation.2 | async-start | bytes 8388608 | tf_op jit(solution)/shard_map/all_to_all | solution.py:574
  121.3 11.6 %own_part.1.base = f32[32,128,256]{2,1,0:T(8,128)} custom-call(s32[1024]{0:T(1024)} %get-tuple-element.14.lists_in.lists, bf16[192,128,256]{2,1,0:T(8,128)(2,1)} %get-tuple-element.16.pairs, bf16[32,128,128]{2,1,0:T(8,128)(2,1)} %get-tuple-element.13.relaid, bf16[32,128,128]{2,1,0:T(8,128)(2,1)} %get-tuple-element.20.mean, ...), custom_call_target="tpu_custom_call" | custom-call | flops 2000000000 | bytes 33554432 | tf_op jit(solution)/shard_map/own_part/pallas_call | solution.py:474
  132.9 41.0 %all-to-all-done.2.far = bf16[128,128,128]{2,1,0:T(8,128)(2,1)} async-done(((bf16[128,128,128]{2,1,0:T(8,128)(2,1)}), bf16[128,128,128]{2,1,0:T(8,128)(2,1)}, u32[]{:S(2)}, u32[]{:S(2)}) %all-to-all-start.2) | async-done | bytes 4194336 | tf_op jit(solution)/shard_map/all_to_all | solution.py:574
  173.9 10.7 %second_layer.1 = bf16[32,128,256]{2,1,0:T(8,128)(2,1)} custom-call(s32[1024]{0:T(1024)} %get-tuple-element.14.lists_in.lists, bf16[128,128,128]{2,1,0:T(8,128)(2,1)} %all-to-all-done.1.remote.near, bf16[128,128,128]{2,1,0:T(8,128)(2,1)} %all-to-all-done.2.far, bf16[192,128,256]{2,1,0:T(8,128)(2,1)} %get-tuple-element.16.pairs, ...), custom_call_target="tpu_custom_call" | custom-call | tf_op jit(solution)/shard_map/second_layer/pallas_call | solution.py:550
Async XLA Ops:
  49.6 58.2 %all-to-all-start.1 = ((bf16[128,128,128]{2,1,0:T(8,128)(2,1)}), bf16[128,128,128]{2,1,0:T(8,128)(2,1)}, u32[]{:S(2)}, u32[]{:S(2)}) async-start(bf16[128,128,128]{2,1,0:T(8,128)(2,1)} %get-tuple-element.15), calls=%async_computation.1 | async-start | bytes 8388608 | tf_op jit(solution)/shard_map/all_to_all | solution.py:574
  116.4 57.6 %all-to-all-start.2 = ((bf16[128,128,128]{2,1,0:T(8,128)(2,1)}), bf16[128,128,128]{2,1,0:T(8,128)(2,1)}, u32[]{:S(2)}, u32[]{:S(2)}) async-start(bf16[128,128,128]{2,1,0:T(8,128)(2,1)} %get-tuple-element.19), calls=%async_computation.2 | async-start | bytes 8388608 | tf_op jit(solution)/shard_map/all_to_all | solution.py:574

commit v4 on v3

--- a/solution.py
+++ b/solution.py
@@ -45,7 +45,10 @@
     return lax.dot_general(a, b, (((1,), (1,)), ((), ())), preferred_element_type=F32)
 
 
-def pack_kernel(owner_in, slot_in, feat, out, rows, held, owner, slot, pos_v, pos_s, sem, sem_feat, sem_owner, sem_slot):
+PARTS = 4
+
+
+def pack_kernel(owner_in, slot_in, feat, out, rows, held, owner, slot, pos_v, pos_s, sems, sem_feat, sem_owner, sem_slot):
     load_owner = pltpu.make_async_copy(owner_in, owner, sem_owner)
     load_slot = pltpu.make_async_copy(slot_in, slot, sem_slot)
     load = pltpu.make_async_copy(feat, held, sem_feat)
@@ -59,6 +62,12 @@
     digits = jnp.zeros((BLK, BLK), F32)
     load_owner.wait()
     load_slot.wait()
+    step = ROWS // BLK // PARTS
+
+    def to_scalar(q):
+        part = pl.ds(q * step, step)
+        return pltpu.make_async_copy(pos_v.at[part], pos_s.at[part], sems.at[q])
+
     for c in range(ROWS // BLK):
         own = owner[c : c + 1, :]
         hit = own == sub
@@ -74,10 +83,9 @@
         spread = jnp.concatenate([hit_f * high, hit_f * low], axis=1).astype(BF)
         ranks = jnp.concatenate([rank_i == sub, rank_i + PER == sub], axis=1).astype(F32).astype(BF)
         digits = digits + mm_t(spread, ranks)
-    copy = pltpu.make_async_copy(pos_v, pos_s, sem)
-    copy.start()
+        if c % step == step - 1:
+            to_scalar(c // step).start()
     rows.reshape(ND, SEG, F)[:, PER:, :] = jnp.broadcast_to(digits[:, None, :], (ND, SEG - PER, F))
-    copy.wait()
     load.wait()
 
     def move(c, _):
@@ -85,14 +93,18 @@
             rows[pl.ds(pos_s[c, u], 1), :] = held[pl.ds(c * BLK + u, 1), :]
         return 0
 
-    lax.fori_loop(0, ROWS // BLK, move, 0)
+    def moves(q, _):
+        to_scalar(q).wait()
+        return lax.fori_loop(q * step, (q + 1) * step, move, 0)
+
+    lax.fori_loop(0, PARTS, moves, 0)
     out[...] = rows[...].reshape(ND, SEG, F).astype(BF)
 
 
 def pack(features, owner, slot):
     return pl.pallas_call(
         pack_kernel,
-        out_shape=jax.ShapeDtypeStruct((ND, SEG, F), BF),
+        out_shape=pltpu.VMEM((ND, SEG, F), BF),
         in_specs=[ANY] * 3,
         out_specs=VMEM,
         scratch_shapes=[
@@ -102,47 +114,51 @@
             pltpu.VMEM((ROWS // BLK, BLK), I32),
             pltpu.VMEM((ROWS // BLK, BLK), I32),
             pltpu.SMEM((ROWS // BLK, BLK), I32),
+            pltpu.SemaphoreType.DMA((PARTS,)),
         ]
-        + [pltpu.SemaphoreType.DMA] * 4,
+        + [pltpu.SemaphoreType.DMA] * 3,
         compiler_params=params(56),
         name="pack",
     )(owner.reshape(ROWS // BLK, BLK), slot.reshape(ROWS // BLK, BLK), features)
 
 
-PARTS = 4
-
-
 def unpack_kernel(
     send_in, arrived, relaid_out, send,
-    send_blocks, held, rows, placed, relaid, slot_v, slot_s, sem, sem_send, sems, sem_relaid, sem_out,
+    send_blocks, rows, placed, relaid, slot_v, slot_s, sem_send, sems, sem_relaid, sem_out,
 ):
-    part = lambda i: pl.ds(i * (ND // PARTS), ND // PARTS)
-    loads = [pltpu.make_async_copy(arrived.at[part(i)], held.at[part(i)], sems.at[i]) for i in range(PARTS)]
     load_send = pltpu.make_async_copy(send_in, send_blocks, sem_send)
-    for load in loads:
-        load.start()
     load_send.start()
-    for i, load in enumerate(loads):
-        load.wait()
-        size = ND // PARTS * SEG
-        rows[pl.ds(i * size, size), :] = held[part(i)].astype(F32).reshape(size, F)
-    digits = rows[pl.ds(PER, ND, stride=SEG), :]
-    slots = digits * 64.0 + pltpu.roll(digits, F - PER, 1)
-    lane = lax.broadcasted_iota(I32, (PER, F), 1)
-    slots = [jnp.where(lane < PER, slots[PER * g : PER * (g + 1)], 0.0) for g in range(ND // PER)]
-    slots = [slots[0]] + [pltpu.roll(slots[g], PER * g, 1) for g in range(1, ND // PER)]
-    slot_v[...] = sum(slots).astype(I32)
-    copy = pltpu.make_async_copy(slot_v, slot_s, sem)
-    copy.start()
-    copy.wait()
-
-    def move(i, _):
-        for u in range(F):
-            source = (i + PER * (u // PER)) * SEG + u % PER
-            placed[pl.ds(slot_s[i, u], 1), :] = rows[pl.ds(source, 1), :]
-        return 0
-
-    lax.fori_loop(0, PER, move, 0)
+    senders = ND // PARTS
+    step = senders * PER // F
+    lane = lax.broadcasted_iota(I32, (step, F), 1)
+
+    def to_scalar(q):
+        part = pl.ds(q * step, step)
+        return pltpu.make_async_copy(slot_v.at[part], slot_s.at[part], sems.at[q])
+
+    for q in range(PARTS):
+        size = senders * SEG
+        rows[pl.ds(q * size, size), :] = arrived[pl.ds(q * senders, senders)].astype(F32).reshape(size, F)
+        digits = rows[pl.ds(q * size + PER, senders, stride=SEG), :]
+        slots = digits * 64.0 + pltpu.roll(digits, F - PER, 1)
+        total = jnp.where(lane < PER, slots[:step], 0.0)
+        for g in range(1, F // PER):
+            total += pltpu.roll(jnp.where(lane < PER, slots[step * g : step * (g + 1)], 0.0), PER * g, 1)
+        slot_v[pl.ds(q * step, step), :] = total.astype(I32)
+        to_scalar(q).start()
+
+    def moves(q, _):
+        to_scalar(q).wait()
+
+        def move(i, _):
+            for u in range(F):
+                source = (q * senders + i + step * (u // PER)) * SEG + u % PER
+                placed[pl.ds(slot_s[q * step + i, u], 1), :] = rows[pl.ds(source, 1), :]
+            return 0
+
+        return lax.fori_loop(0, step, move, 0)
+
+    lax.fori_loop(0, PARTS, moves, 0)
     relaid[...] = placed[...].reshape(NB, BLK, F).astype(BF)
     load_send.wait()
 
@@ -161,20 +177,18 @@
     return pl.pallas_call(
         unpack_kernel,
         out_shape=(
-            jax.ShapeDtypeStruct((NB, BLK, F), BF),
-            jax.ShapeDtypeStruct((ND, BLK, F), BF),
+            pltpu.HBM((NB, BLK, F), BF),
+            pltpu.HBM((ND, BLK, F), BF),
         ),
-        in_specs=[ANY, ANY],
+        in_specs=[ANY, VMEM],
         out_specs=(ANY, ANY),
         scratch_shapes=[
             pltpu.SMEM((ND,), I32),
-            pltpu.VMEM((ND, SEG, F), BF),
             pltpu.VMEM((ND * SEG, F), F32),
             pltpu.VMEM((ROWS, F), F32),
             pltpu.VMEM((NB, BLK, F), BF),
             pltpu.VMEM((PER, F), I32),
             pltpu.SMEM((PER, F), I32),
-            pltpu.SemaphoreType.DMA,
             pltpu.SemaphoreType.DMA,
             pltpu.SemaphoreType.DMA((PARTS,)),
             pltpu.SemaphoreType.DMA,
@@ -579,7 +593,8 @@
     w_self1, w_neigh1, w_self2, w_neigh2,
 ):
     picks = send_blocks.reshape(ND)
-    arrived = exchange(pack(features, owner, slot))
+    features = pltpu.with_memory_space_constraint(features, pltpu.HBM)
+    arrived = pltpu.with_memory_space_constraint(exchange(pack(features, owner, slot)), pltpu.VMEM)
     relaid, send = unpack(picks, arrived)
     near = exchange(send)
     pairs, base, inv, lists = prepare(tile_row, tile_col, tile_count, picks, tile_vals, relaid)

time: 185 us -> 182 us (0.984)
  Pallas kernels: 74.2 us -> 70.3 us
    pallas_call x2, Pallas kernels: 15.8 us -> 12.9 us  [the longest x1 6.77 us: unpack(): pl.pallas_call(unpack_kernel, out_shape=(pltpu.HBM((NB, BLK, F), BF), plt...]
  transfers between devices with their start and end apart: 2 -> 2, of which waited for: 2 -> 2; matrix products, arithmetic and copies ran while one was open for 0% -> 0% of each run, Pallas kernels for 21% -> 22%
where the time goes in v4:
time: 182 us; the launch traced here: 181 us
  Pallas kernels  70.3 us (39%)
  waiting for transfers between devices  65.6 us (36%)
  blocking collectives  33.5 us (18%)
  starting transfers between devices  10.9 us (6%)
    all_to_all x2, waiting for transfers between devices, exchange(): return lax.all_to_all(x, 'dom', split_axis=0, concat_axis=0, tiled=True)  65.6 us
    all_to_all x1, blocking collectives, exchange(): return lax.all_to_all(x, 'dom', split_axis=0, concat_axis=0, tiled=True)  33.5 us
    pallas_call x1, Pallas kernels, prepare(): pl.pallas_call(prepare_kernel, out_shape=(jax.ShapeDtypeStruct((PAIRS, BL...  27 us
    pallas_call x1, Pallas kernels, own_part(): pl.pallas_call(own_kernel, out_shape=jax.ShapeDtypeStruct((NB, BLK, H), F...  12.2 us
    all_to_all x2, starting transfers between devices, exchange(): return lax.all_to_all(x, 'dom', split_axis=0, concat_axis=0, tiled=True)  10.9 us
    pallas_call x1, Pallas kernels, second(): pl.pallas_call(second_kernel, out_shape=jax.ShapeDtypeStruct((NB, BLK, H)...  10.2 us
    pallas_call x1, Pallas kernels, first(): pl.pallas_call(first_kernel, out_shape=(jax.ShapeDtypeStruct((NB, BLK, F)...  8.07 us
    pallas_call x1, Pallas kernels, unpack(): pl.pallas_call(unpack_kernel, out_shape=(pltpu.HBM((NB, BLK, F), BF), plt...  6.77 us
  transfers between devices with their start and end apart: 2, of which 2 were waited for; matrix products, arithmetic and copies ran while one was open for 0% of the time, Pallas kernels for 22%

profile of v4, /device:TPU:1, one launch (start us, length us, event | category | flops | bytes accessed | tf_op | source)
XLA Modules:
  0.0 181.0 jit_solution(1113362043099539895)
XLA Ops:
  0.0 6.1 %pack.1 = bf16[128,40,128]{2,1,0:T(8,128)(2,1)S(1)} custom-call(s32[32,128]{1,0:T(8,128)} %bitcast.4, s32[32,128]{1,0:T(8,128)} %bitcast.5, f32[4096,128]{1,0:T(8,128)} %feat.1), custom_call_target="tpu_custom_call" | custom-call | tf_op jit(solution)/shard_map/pack/pallas_call | solution.py:105
  6.1 33.5 %all_to_all.15.arrived = bf16[128,40,128]{2,1,0:T(8,128)(2,1)S(1)} all-to-all(bf16[128,40,128]{2,1,0:T(8,128)(2,1)S(1)} %pack.1), channel_id=1, replica_groups=mesh['dom'=128] {'dom'}, dimensions={0} | all-to-all | bytes 2621440 | tf_op jit(solution)/shard_map/all_to_all | solution.py:588
  39.6 6.8 %unpack.1 = (bf16[32,128,128]{2,1,0:T(8,128)(2,1)}, bf16[128,128,128]{2,1,0:T(8,128)(2,1)}) custom-call(s32[128]{0:T(128)} %bitcast.6, bf16[128,40,128]{2,1,0:T(8,128)(2,1)S(1)} %all_to_all.15.arrived), custom_call_target="tpu_custom_call" | custom-call | tf_op jit(solution)/shard_map/unpack/pallas_call | solution.py:177
  46.3 5.4 %all-to-all-start.1 = ((bf16[128,128,128]{2,1,0:T(8,128)(2,1)}), bf16[128,128,128]{2,1,0:T(8,128)(2,1)}, u32[]{:S(2)}, u32[]{:S(2)}) async-start(bf16[128,128,128]{2,1,0:T(8,128)(2,1)} %get-tuple-element.15), calls=%async_computation.1 | async-start | bytes 8388608 | tf_op jit(solution)/shard_map/all_to_all | solution.py:588
  52.4 27.0 %prepare.1 = (bf16[192,128,256]{2,1,0:T(8,128)(2,1)}, f32[32,128,128]{2,1,0:T(8,128)}, f32[32,128,128]{2,1,0:T(8,128)}, s32[1024]{0:T(1024)}) custom-call(s32[256]{0:T(256)} %row_s.1, s32[256]{0:T(256)} %col_s.1, s32[1]{0:T(128)S(6)} %copy.13.count_s, s32[128]{0:T(128)} %bitcast.7, s32[256,128,128]{2,1,0:T(8,128)} %tile_vals.1, ...), custom_call_target="tpu_custom_call" | custom-call | flops 2000000000 | bytes 33554432 | tf_op jit(solution)/shard_map/prepare/pallas_call | solution.py:325
  79.4 25.1 %all-to-all-done.1.remote.near = bf16[128,128,128]{2,1,0:T(8,128)(2,1)} async-done(((bf16[128,128,128]{2,1,0:T(8,128)(2,1)}), bf16[128,128,128]{2,1,0:T(8,128)(2,1)}, u32[]{:S(2)}, u32[]{:S(2)}) %all-to-all-start.1) | async-done | bytes 4194336 | tf_op jit(solution)/shard_map/all_to_all | solution.py:588
  104.6 8.1 %first_layer.1 = (bf16[32,128,128]{2,1,0:T(8,128)(2,1)}, bf16[128,128,128]{2,1,0:T(8,128)(2,1)}) custom-call(s32[1024]{0:T(1024)} %get-tuple-element.14.lists_in.lists, bf16[128,128,128]{2,1,0:T(8,128)(2,1)} %all-to-all-done.1.remote.near, bf16[192,128,256]{2,1,0:T(8,128)(2,1)} %get-tuple-element.16.pairs, f32[32,128,128]{2,1,0:T(8,128)} %get-tuple-element.17.base, ...), custom_call_target="tpu_custom_call" | custom-call | tf_op jit(solution)/shard_map/first_layer/pallas_call | solution.py:431
  112.7 5.4 %all-to-all-start.2 = ((bf16[128,128,128]{2,1,0:T(8,128)(2,1)}), bf16[128,128,128]{2,1,0:T(8,128)(2,1)}, u32[]{:S(2)}, u32[]{:S(2)}) async-start(bf16[128,128,128]{2,1,0:T(8,128)(2,1)} %get-tuple-element.19), calls=%async_computation.2 | async-start | bytes 8388608 | tf_op jit(solution)/shard_map/all_to_all | solution.py:588
  118.1 12.2 %own_part.1.base = f32[32,128,256]{2,1,0:T(8,128)} custom-call(s32[1024]{0:T(1024)} %get-tuple-element.14.lists_in.lists, bf16[192,128,256]{2,1,0:T(8,128)(2,1)} %get-tuple-element.16.pairs, bf16[32,128,128]{2,1,0:T(8,128)(2,1)} %get-tuple-element.13.relaid, bf16[32,128,128]{2,1,0:T(8,128)(2,1)} %get-tuple-element.20.mean, ...), custom_call_target="tpu_custom_call" | custom-call | flops 2000000000 | bytes 33554432 | tf_op jit(solution)/shard_map/own_part/pallas_call | solution.py:488
  130.3 40.5 %all-to-all-done.2.far = bf16[128,128,128]{2,1,0:T(8,128)(2,1)} async-done(((bf16[128,128,128]{2,1,0:T(8,128)(2,1)}), bf16[128,128,128]{2,1,0:T(8,128)(2,1)}, u32[]{:S(2)}, u32[]{:S(2)}) %all-to-all-start.2) | async-done | bytes 4194336 | tf_op jit(solution)/shard_map/all_to_all | solution.py:588
  170.7 10.2 %second_layer.1 = bf16[32,128,256]{2,1,0:T(8,128)(2,1)} custom-call(s32[1024]{0:T(1024)} %get-tuple-element.14.lists_in.lists, bf16[128,128,128]{2,1,0:T(8,128)(2,1)} %all-to-all-done.1.remote.near, bf16[128,128,128]{2,1,0:T(8,128)(2,1)} %all-to-all-done.2.far, bf16[192,128,256]{2,1,0:T(8,128)(2,1)} %get-tuple-element.16.pairs, ...), custom_call_target="tpu_custom_call" | custom-call | tf_op jit(solution)/shard_map/second_layer/pallas_call | solution.py:564
Async XLA Ops:
  46.3 58.2 %all-to-all-start.1 = ((bf16[128,128,128]{2,1,0:T(8,128)(2,1)}), bf16[128,128,128]{2,1,0:T(8,128)(2,1)}, u32[]{:S(2)}, u32[]{:S(2)}) async-start(bf16[128,128,128]{2,1,0:T(8,128)(2,1)} %get-tuple-element.15), calls=%async_computation.1 | async-start | bytes 8388608 | tf_op jit(solution)/shard_map/all_to_all | solution.py:588
  112.7 58.1 %all-to-all-start.2 = ((bf16[128,128,128]{2,1,0:T(8,128)(2,1)}), bf16[128,128,128]{2,1,0:T(8,128)(2,1)}, u32[]{:S(2)}, u32[]{:S(2)}) async-start(bf16[128,128,128]{2,1,0:T(8,128)(2,1)} %get-tuple-element.19), calls=%async_computation.2 | async-start | bytes 8388608 | tf_op jit(solution)/shard_map/all_to_all | solution.py:588

commit v5 on v4

--- a/solution.py
+++ b/solution.py
@@ -13,7 +13,7 @@
 NB = 32
 ND = 128
 PER = ROWS // ND
-SEG = PER + 8
+SEG = PER + 2
 PAIRS = 192
 GROUP = 16
 BATCH = 8
@@ -85,7 +85,8 @@
         digits = digits + mm_t(spread, ranks)
         if c % step == step - 1:
             to_scalar(c // step).start()
-    rows.reshape(ND, SEG, F)[:, PER:, :] = jnp.broadcast_to(digits[:, None, :], (ND, SEG - PER, F))
+    for extra in range(PER, SEG):
+        rows[pl.ds(extra, ND, stride=SEG), :] = digits
     load.wait()
 
     def move(c, _):
@@ -98,13 +99,13 @@
         return lax.fori_loop(q * step, (q + 1) * step, move, 0)
 
     lax.fori_loop(0, PARTS, moves, 0)
-    out[...] = rows[...].reshape(ND, SEG, F).astype(BF)
+    out[...] = rows[...].astype(BF)
 
 
 def pack(features, owner, slot):
     return pl.pallas_call(
         pack_kernel,
-        out_shape=pltpu.VMEM((ND, SEG, F), BF),
+        out_shape=pltpu.VMEM((ND * SEG, F), BF),
         in_specs=[ANY] * 3,
         out_specs=VMEM,
         scratch_shapes=[
@@ -138,7 +139,7 @@
 
     for q in range(PARTS):
         size = senders * SEG
-        rows[pl.ds(q * size, size), :] = arrived[pl.ds(q * senders, senders)].astype(F32).reshape(size, F)
+        rows[pl.ds(q * size, size), :] = arrived[pl.ds(q * size, size), :].astype(F32)
         digits = rows[pl.ds(q * size + PER, senders, stride=SEG), :]
         slots = digits * 64.0 + pltpu.roll(digits, F - PER, 1)
         total = jnp.where(lane < PER, slots[:step], 0.0)
@@ -594,7 +595,8 @@
 ):
     picks = send_blocks.reshape(ND)
     features = pltpu.with_memory_space_constraint(features, pltpu.HBM)
-    arrived = pltpu.with_memory_space_constraint(exchange(pack(features, owner, slot)), pltpu.VMEM)
+    packed = pack(features, owner, slot).reshape(ND, SEG // 2, 2, F)
+    arrived = pltpu.with_memory_space_constraint(exchange(packed).reshape(ND * SEG, F), pltpu.VMEM)
     relaid, send = unpack(picks, arrived)
     near = exchange(send)
     pairs, base, inv, lists = prepare(tile_row, tile_col, tile_count, picks, tile_vals, relaid)

time: 182 us -> 179 us (0.984)
  Pallas kernels: 70.3 us -> 68.1 us
  waiting for transfers between devices: 65.6 us -> 67.8 us
  blocking collectives: 33.5 us -> 31.3 us
    all_to_all x2, waiting for transfers between devices: 65.6 us -> 67.8 us  [exchange(): return lax.all_to_all(x, 'dom', split_axis=0, concat_axis=0, tiled=True)]
    all_to_all x1, blocking collectives: 33.5 us -> 31.3 us  [exchange(): return lax.all_to_all(x, 'dom', split_axis=0, concat_axis=0, tiled=True)]
  transfers between devices with their start and end apart: 2 -> 2, of which waited for: 2 -> 2; matrix products, arithmetic and copies ran while one was open for 0% -> 0% of each run, Pallas kernels for 22% -> 21%
where the time goes in v5:
time: 179 us
  Pallas kernels  68.1 us (38%)
  waiting for transfers between devices  67.8 us (38%)
  blocking collectives  31.3 us (17%)
  starting transfers between devices  10.9 us (6%)
    all_to_all x2, waiting for transfers between devices, exchange(): return lax.all_to_all(x, 'dom', split_axis=0, concat_axis=0, tiled=True)  67.8 us
    all_to_all x1, blocking collectives, exchange(): return lax.all_to_all(x, 'dom', split_axis=0, concat_axis=0, tiled=True)  31.3 us
    pallas_call x1, Pallas kernels, prepare(): pl.pallas_call(prepare_kernel, out_shape=(jax.ShapeDtypeStruct((PAIRS, BL...  25.3 us
    pallas_call x1, Pallas kernels, own_part(): pl.pallas_call(own_kernel, out_shape=jax.ShapeDtypeStruct((NB, BLK, H), F...  11.6 us
    all_to_all x2, starting transfers between devices, exchange(): return lax.all_to_all(x, 'dom', split_axis=0, concat_axis=0, tiled=True)  10.9 us
    pallas_call x1, Pallas kernels, second(): pl.pallas_call(second_kernel, out_shape=jax.ShapeDtypeStruct((NB, BLK, H)...  10.2 us
    pallas_call x1, Pallas kernels, first(): pl.pallas_call(first_kernel, out_shape=(jax.ShapeDtypeStruct((NB, BLK, F)...  8.09 us
    pallas_call x1, Pallas kernels, unpack(): pl.pallas_call(unpack_kernel, out_shape=(pltpu.HBM((NB, BLK, F), BF), plt...  6.73 us
  transfers between devices with their start and end apart: 2, of which 2 were waited for; matrix products, arithmetic and copies ran while one was open for 0% of the time, Pallas kernels for 21%

profile of v5, /device:TPU:1, one launch (start us, length us, event | category | flops | bytes accessed | tf_op | source)
XLA Modules:
  0.0 178.8 jit_solution(15564502375493286347)
XLA Ops:
  0.0 6.1 %pack.1 = bf16[4352,128]{1,0:T(8,128)(2,1)S(1)} custom-call(s32[32,128]{1,0:T(8,128)} %bitcast.8, s32[32,128]{1,0:T(8,128)} %bitcast.9, f32[4096,128]{1,0:T(8,128)} %feat.1), custom_call_target="tpu_custom_call" | custom-call | tf_op jit(solution)/shard_map/pack/pallas_call | solution.py:106
  6.1 31.3 %all_to_all.15 = bf16[128,17,2,128]{3,2,1,0:T(2,128)(2,1)S(1)} all-to-all(bf16[128,17,2,128]{3,2,1,0:T(2,128)(2,1)S(1)} %bitcast.7), channel_id=1, replica_groups=mesh['dom'=128] {'dom'}, dimensions={0} | all-to-all | bytes 2228224 | tf_op jit(solution)/shard_map/all_to_all | solution.py:589
  37.4 6.7 %unpack.1 = (bf16[32,128,128]{2,1,0:T(8,128)(2,1)}, bf16[128,128,128]{2,1,0:T(8,128)(2,1)}) custom-call(s32[128]{0:T(128)} %bitcast.10, bf16[4352,128]{1,0:T(8,128)(2,1)S(1)} %bitcast.6), custom_call_target="tpu_custom_call" | custom-call | tf_op jit(solution)/shard_map/unpack/pallas_call | solution.py:178
  44.2 5.4 %all-to-all-start.1 = ((bf16[128,128,128]{2,1,0:T(8,128)(2,1)}), bf16[128,128,128]{2,1,0:T(8,128)(2,1)}, u32[]{:S(2)}, u32[]{:S(2)}) async-start(bf16[128,128,128]{2,1,0:T(8,128)(2,1)} %get-tuple-element.15), calls=%async_computation.1 | async-start | bytes 8388608 | tf_op jit(solution)/shard_map/all_to_all | solution.py:589
  50.3 25.3 %prepare.1 = (bf16[192,128,256]{2,1,0:T(8,128)(2,1)}, f32[32,128,128]{2,1,0:T(8,128)}, f32[32,128,128]{2,1,0:T(8,128)}, s32[1024]{0:T(1024)}) custom-call(s32[256]{0:T(256)} %row_s.1, s32[256]{0:T(256)} %col_s.1, s32[1]{0:T(128)S(6)} %copy.13.count_s, s32[128]{0:T(128)} %bitcast.11, s32[256,128,128]{2,1,0:T(8,128)} %tile_vals.1, ...), custom_call_target="tpu_custom_call" | custom-call | flops 2000000000 | bytes 33554432 | tf_op jit(solution)/shard_map/prepare/pallas_call | solution.py:326
  75.6 26.8 %all-to-all-done.1.remote.near = bf16[128,128,128]{2,1,0:T(8,128)(2,1)} async-done(((bf16[128,128,128]{2,1,0:T(8,128)(2,1)}), bf16[128,128,128]{2,1,0:T(8,128)(2,1)}, u32[]{:S(2)}, u32[]{:S(2)}) %all-to-all-start.1) | async-done | bytes 4194336 | tf_op jit(solution)/shard_map/all_to_all | solution.py:589
  102.4 8.1 %first_layer.1 = (bf16[32,128,128]{2,1,0:T(8,128)(2,1)}, bf16[128,128,128]{2,1,0:T(8,128)(2,1)}) custom-call(s32[1024]{0:T(1024)} %get-tuple-element.14.lists_in.lists, bf16[128,128,128]{2,1,0:T(8,128)(2,1)} %all-to-all-done.1.remote.near, bf16[192,128,256]{2,1,0:T(8,128)(2,1)} %get-tuple-element.16.pairs, f32[32,128,128]{2,1,0:T(8,128)} %get-tuple-element.17.base, ...), custom_call_target="tpu_custom_call" | custom-call | tf_op jit(solution)/shard_map/first_layer/pallas_call | solution.py:432
  110.5 5.4 %all-to-all-start.2 = ((bf16[128,128,128]{2,1,0:T(8,128)(2,1)}), bf16[128,128,128]{2,1,0:T(8,128)(2,1)}, u32[]{:S(2)}, u32[]{:S(2)}) async-start(bf16[128,128,128]{2,1,0:T(8,128)(2,1)} %get-tuple-element.19), calls=%async_computation.2 | async-start | bytes 8388608 | tf_op jit(solution)/shard_map/all_to_all | solution.py:589
  115.9 11.6 %own_part.1.base = f32[32,128,256]{2,1,0:T(8,128)} custom-call(s32[1024]{0:T(1024)} %get-tuple-element.14.lists_in.lists, bf16[192,128,256]{2,1,0:T(8,128)(2,1)} %get-tuple-element.16.pairs, bf16[32,128,128]{2,1,0:T(8,128)(2,1)} %get-tuple-element.13.relaid, bf16[32,128,128]{2,1,0:T(8,128)(2,1)} %get-tuple-element.20.mean, ...), custom_call_target="tpu_custom_call" | custom-call | flops 2000000000 | bytes 33554432 | tf_op jit(solution)/shard_map/own_part/pallas_call | solution.py:489
  127.6 41.0 %all-to-all-done.2.far = bf16[128,128,128]{2,1,0:T(8,128)(2,1)} async-done(((bf16[128,128,128]{2,1,0:T(8,128)(2,1)}), bf16[128,128,128]{2,1,0:T(8,128)(2,1)}, u32[]{:S(2)}, u32[]{:S(2)}) %all-to-all-start.2) | async-done | bytes 4194336 | tf_op jit(solution)/shard_map/all_to_all | solution.py:589
  168.6 10.2 %second_layer.1 = bf16[32,128,256]{2,1,0:T(8,128)(2,1)} custom-call(s32[1024]{0:T(1024)} %get-tuple-element.14.lists_in.lists, bf16[128,128,128]{2,1,0:T(8,128)(2,1)} %all-to-all-done.1.remote.near, bf16[128,128,128]{2,1,0:T(8,128)(2,1)} %all-to-all-done.2.far, bf16[192,128,256]{2,1,0:T(8,128)(2,1)} %get-tuple-element.16.pairs, ...), custom_call_target="tpu_custom_call" | custom-call | tf_op jit(solution)/shard_map/second_layer/pallas_call | solution.py:565
Async XLA Ops:
  44.2 58.2 %all-to-all-start.1 = ((bf16[128,128,128]{2,1,0:T(8,128)(2,1)}), bf16[128,128,128]{2,1,0:T(8,128)(2,1)}, u32[]{:S(2)}, u32[]{:S(2)}) async-start(bf16[128,128,128]{2,1,0:T(8,128)(2,1)} %get-tuple-element.15), calls=%async_computation.1 | async-start | bytes 8388608 | tf_op jit(solution)/shard_map/all_to_all | solution.py:589
  110.5 58.1 %all-to-all-start.2 = ((bf16[128,128,128]{2,1,0:T(8,128)(2,1)}), bf16[128,128,128]{2,1,0:T(8,128)(2,1)}, u32[]{:S(2)}, u32[]{:S(2)}) async-start(bf16[128,128,128]{2,1,0:T(8,128)(2,1)} %get-tuple-element.19), calls=%async_computation.2 | async-start | bytes 8388608 | tf_op jit(solution)/shard_map/all_to_all | solution.py:589

commit v6 on v5

--- a/solution.py
+++ b/solution.py
@@ -45,6 +45,7 @@
     return lax.dot_general(a, b, (((1,), (1,)), ((), ())), preferred_element_type=F32)
 
 
+POSTS = 16
 PARTS = 4
 
 
@@ -163,11 +164,13 @@
     relaid[...] = placed[...].reshape(NB, BLK, F).astype(BF)
     load_send.wait()
 
-    def post(d, _):
-        pltpu.make_async_copy(relaid.at[send_blocks[d]], send.at[d], sem_out).start()
-        return 0
-
-    lax.fori_loop(0, ND, post, 0)
+    def post(i, _):
+        for u in range(POSTS):
+            d = i * POSTS + u
+            pltpu.make_async_copy(relaid.at[send_blocks[d]], send.at[d], sem_out).start()
+        return 0
+
+    lax.fori_loop(0, ND // POSTS, post, 0)
     keep = pltpu.make_async_copy(relaid, relaid_out, sem_relaid)
     keep.start()
     pltpu.make_async_copy(send, send, sem_out).wait()

time: 179 us -> 178 us (level)
  Pallas kernels: 68.1 us -> 61.3 us
  waiting for transfers between devices: 67.8 us -> 73 us
    all_to_all x2, waiting for transfers between devices: 67.8 us -> 73 us  [exchange(): return lax.all_to_all(x, 'dom', split_axis=0, concat_axis=0, tiled=True)]
    pallas_call x1, Pallas kernels: 25.3 us -> 20.8 us  [prepare(): pl.pallas_call(prepare_kernel, out_shape=(jax.ShapeDtypeStruct((PAIRS, BL...]
  transfers between devices with their start and end apart: 2 -> 2, of which waited for: 2 -> 2; matrix products, arithmetic and copies ran while one was open for 0% -> 0% of each run, Pallas kernels for 21% -> 18%
where the time goes in v6:
time: 178 us
  waiting for transfers between devices  73 us (41%)
  Pallas kernels  61.3 us (34%)
  blocking collectives  31.3 us (18%)
  starting transfers between devices  11.4 us (6%)
    all_to_all x2, waiting for transfers between devices, exchange(): return lax.all_to_all(x, 'dom', split_axis=0, concat_axis=0, tiled=True)  73 us
    all_to_all x1, blocking collectives, exchange(): return lax.all_to_all(x, 'dom', split_axis=0, concat_axis=0, tiled=True)  31.3 us
    pallas_call x1, Pallas kernels, prepare(): pl.pallas_call(prepare_kernel, out_shape=(jax.ShapeDtypeStruct((PAIRS, BL...  20.8 us
    all_to_all x2, starting transfers between devices, exchange(): return lax.all_to_all(x, 'dom', split_axis=0, concat_axis=0, tiled=True)  11.4 us
    pallas_call x1, Pallas kernels, own_part(): pl.pallas_call(own_kernel, out_shape=jax.ShapeDtypeStruct((NB, BLK, H), F...  11.1 us
    pallas_call x1, Pallas kernels, second(): pl.pallas_call(second_kernel, out_shape=jax.ShapeDtypeStruct((NB, BLK, H)...  9.21 us
    pallas_call x1, Pallas kernels, first(): pl.pallas_call(first_kernel, out_shape=(jax.ShapeDtypeStruct((NB, BLK, F)...  7.35 us
    pallas_call x1, Pallas kernels, unpack(): pl.pallas_call(unpack_kernel, out_shape=(pltpu.HBM((NB, BLK, F), BF), plt...  6.73 us
  transfers between devices with their start and end apart: 2, of which 2 were waited for; matrix products, arithmetic and copies ran while one was open for 0% of the time, Pallas kernels for 18%

profile of v6, /device:TPU:1, one launch (start us, length us, event | category | flops | bytes accessed | tf_op | source)
XLA Modules:
  0.0 177.7 jit_solution(6226989999092746148)
XLA Ops:
  0.0 6.1 %pack.1 = bf16[4352,128]{1,0:T(8,128)(2,1)S(1)} custom-call(s32[32,128]{1,0:T(8,128)} %bitcast.8, s32[32,128]{1,0:T(8,128)} %bitcast.9, f32[4096,128]{1,0:T(8,128)} %feat.1), custom_call_target="tpu_custom_call" | custom-call | tf_op jit(solution)/shard_map/pack/pallas_call | solution.py:107
  6.1 31.3 %all_to_all.15 = bf16[128,17,2,128]{3,2,1,0:T(2,128)(2,1)S(1)} all-to-all(bf16[128,17,2,128]{3,2,1,0:T(2,128)(2,1)S(1)} %bitcast.7), channel_id=1, replica_groups=mesh['dom'=128] {'dom'}, dimensions={0} | all-to-all | bytes 2228224 | tf_op jit(solution)/shard_map/all_to_all | solution.py:592
  37.4 6.7 %unpack.1 = (bf16[32,128,128]{2,1,0:T(8,128)(2,1)}, bf16[128,128,128]{2,1,0:T(8,128)(2,1)}) custom-call(s32[128]{0:T(128)} %bitcast.10, bf16[4352,128]{1,0:T(8,128)(2,1)S(1)} %bitcast.6), custom_call_target="tpu_custom_call" | custom-call | tf_op jit(solution)/shard_map/unpack/pallas_call | solution.py:181
  44.2 5.4 %all-to-all-start.1 = ((bf16[128,128,128]{2,1,0:T(8,128)(2,1)}), bf16[128,128,128]{2,1,0:T(8,128)(2,1)}, u32[]{:S(2)}, u32[]{:S(2)}) async-start(bf16[128,128,128]{2,1,0:T(8,128)(2,1)} %get-tuple-element.15), calls=%async_computation.1 | async-start | bytes 8388608 | tf_op jit(solution)/shard_map/all_to_all | solution.py:592
  50.3 20.8 %prepare.1 = (bf16[192,128,256]{2,1,0:T(8,128)(2,1)}, f32[32,128,128]{2,1,0:T(8,128)}, f32[32,128,128]{2,1,0:T(8,128)}, s32[1024]{0:T(1024)}) custom-call(s32[256]{0:T(256)} %row_s.1, s32[256]{0:T(256)} %col_s.1, s32[1]{0:T(128)S(6)} %copy.13.count_s, s32[128]{0:T(128)} %bitcast.11, s32[256,128,128]{2,1,0:T(8,128)} %tile_vals.1, ...), custom_call_target="tpu_custom_call" | custom-call | flops 2000000000 | bytes 33554432 | tf_op jit(solution)/shard_map/prepare/pallas_call | solution.py:329
  71.0 31.4 %all-to-all-done.1.remote.near = bf16[128,128,128]{2,1,0:T(8,128)(2,1)} async-done(((bf16[128,128,128]{2,1,0:T(8,128)(2,1)}), bf16[128,128,128]{2,1,0:T(8,128)(2,1)}, u32[]{:S(2)}, u32[]{:S(2)}) %all-to-all-start.1) | async-done | bytes 4194336 | tf_op jit(solution)/shard_map/all_to_all | solution.py:592
  102.4 7.3 %first_layer.1 = (bf16[32,128,128]{2,1,0:T(8,128)(2,1)}, bf16[128,128,128]{2,1,0:T(8,128)(2,1)}) custom-call(s32[1024]{0:T(1024)} %get-tuple-element.14.lists_in.lists, bf16[128,128,128]{2,1,0:T(8,128)(2,1)} %all-to-all-done.1.remote.near, bf16[192,128,256]{2,1,0:T(8,128)(2,1)} %get-tuple-element.16.pairs, f32[32,128,128]{2,1,0:T(8,128)} %get-tuple-element.17.base, ...), custom_call_target="tpu_custom_call" | custom-call | tf_op jit(solution)/shard_map/first_layer/pallas_call | solution.py:435
  109.8 5.9 %all-to-all-start.2 = ((bf16[128,128,128]{2,1,0:T(8,128)(2,1)}), bf16[128,128,128]{2,1,0:T(8,128)(2,1)}, u32[]{:S(2)}, u32[]{:S(2)}) async-start(bf16[128,128,128]{2,1,0:T(8,128)(2,1)} %get-tuple-element.19), calls=%async_computation.2 | async-start | bytes 8388608 | tf_op jit(solution)/shard_map/all_to_all | solution.py:592
  115.7 11.1 %own_part.1.base = f32[32,128,256]{2,1,0:T(8,128)} custom-call(s32[1024]{0:T(1024)} %get-tuple-element.14.lists_in.lists, bf16[192,128,256]{2,1,0:T(8,128)(2,1)} %get-tuple-element.16.pairs, bf16[32,128,128]{2,1,0:T(8,128)(2,1)} %get-tuple-element.13.relaid, bf16[32,128,128]{2,1,0:T(8,128)(2,1)} %get-tuple-element.20.mean, ...), custom_call_target="tpu_custom_call" | custom-call | flops 2000000000 | bytes 33554432 | tf_op jit(solution)/shard_map/own_part/pallas_call | solution.py:492
  126.9 41.6 %all-to-all-done.2.far = bf16[128,128,128]{2,1,0:T(8,128)(2,1)} async-done(((bf16[128,128,128]{2,1,0:T(8,128)(2,1)}), bf16[128,128,128]{2,1,0:T(8,128)(2,1)}, u32[]{:S(2)}, u32[]{:S(2)}) %all-to-all-start.2) | async-done | bytes 4194336 | tf_op jit(solution)/shard_map/all_to_all | solution.py:592
  168.5 9.2 %second_layer.1 = bf16[32,128,256]{2,1,0:T(8,128)(2,1)} custom-call(s32[1024]{0:T(1024)} %get-tuple-element.14.lists_in.lists, bf16[128,128,128]{2,1,0:T(8,128)(2,1)} %all-to-all-done.1.remote.near, bf16[128,128,128]{2,1,0:T(8,128)(2,1)} %all-to-all-done.2.far, bf16[192,128,256]{2,1,0:T(8,128)(2,1)} %get-tuple-element.16.pairs, ...), custom_call_target="tpu_custom_call" | custom-call | tf_op jit(solution)/shard_map/second_layer/pallas_call | solution.py:568
Async XLA Ops:
  44.2 58.2 %all-to-all-start.1 = ((bf16[128,128,128]{2,1,0:T(8,128)(2,1)}), bf16[128,128,128]{2,1,0:T(8,128)(2,1)}, u32[]{:S(2)}, u32[]{:S(2)}) async-start(bf16[128,128,128]{2,1,0:T(8,128)(2,1)} %get-tuple-element.15), calls=%async_computation.1 | async-start | bytes 8388608 | tf_op jit(solution)/shard_map/all_to_all | solution.py:592
  109.8 58.7 %all-to-all-start.2 = ((bf16[128,128,128]{2,1,0:T(8,128)(2,1)}), bf16[128,128,128]{2,1,0:T(8,128)(2,1)}, u32[]{:S(2)}, u32[]{:S(2)}) async-start(bf16[128,128,128]{2,1,0:T(8,128)(2,1)} %get-tuple-element.19), calls=%async_computation.2 | async-start | bytes 8388608 | tf_op jit(solution)/shard_map/all_to_all | solution.py:592
